TPU v7x, 256 devices: a whole 4x4x8 slice. The times are simulated.
256 devices in a mesh: pipe: 8 (over z), sp: 16 (over y_hi, x, core), cfg: 2 (over y_lo).
Axes of the slice: x: 4, y: 4 (y_hi: 2, y_lo: 2; y = y_hi * 2 + y_lo), z: 8, core: 2. Of those that a mesh axis runs over, the one named last changes fastest.
Arguments:
- patch_tokens: bfloat16 [4, 128, 3072], P(None, 'sp'), may hold values from -6 to 6
- modulation: float32 [8, 2, 3, 3072], P('pipe', 'cfg'), may hold values from -3 to 3
- w_qkv: bfloat16 [8, 3072, 3, 2048], P('pipe', None, None, 'sp'), may hold values from -1 to 1
- qk_gain: float32 [8, 2, 128], P('pipe'), may hold values from 0.5 to 8
- w_out: bfloat16 [8, 2048, 3072], P('pipe', 'sp'), may hold values from -0.125 to 0.125
- kv_cache: bfloat16 [8, 2, 2, 8192, 2048], P('pipe', 'cfg', None, None, 'sp'), may hold values from -6 to 6
- order: int32 [64], replicated, may hold values from 0 to 63, each once
- offsets: int32 [64], replicated, may hold values from 0 to 8064, as said below
Outputs:
- section_out: bfloat16 [8, 2, 4, 128, 3072], P('pipe', 'cfg', None, 'sp')
- guided: bfloat16 [4, 128, 3072], P('cfg', 'sp', 'pipe')
Inputs may be any that keep to these rules, and one draw needn't show every extreme that they name: `order`: the first 4 entries name the window's patches. `offsets`: distinct multiples of 128, one for each image patch.
All inputs are finite; a program needn't handle non-finite values.
Results may differ from a plain program's by a relative error of at most 0.035.
Values may be sent and summed in bfloat16 or wider, within the bound.
No kernel may reach another device: no remote copies, remote signals or barrier semaphores. Data moves between devices by JAX's collectives and lax.ppermute only.
A program may use at most 128 MiB of HBM per device.

v0:
```python
import math

import jax
import jax.numpy as jnp
from jax import lax
from jax.sharding import PartitionSpec as P

HD = 128


norm_eps = 1e-06
guide_scale = 3.5


def from_behind(block, axis, distance):
    devices = range(lax.axis_size(axis))
    route = [(i - distance, i) for i in devices if i - distance in devices]
    return lax.ppermute(block, axis, route)


def from_partner(value, axis, apart):
    mask = 2**apart
    pairs = [(source, source ^ mask) for source in range(lax.axis_size(axis))]
    return lax.ppermute(value, axis, pairs)


def spread(block, axis, owner):
    block = jnp.where(lax.axis_index(axis) == owner, block, jnp.zeros_like(block))
    return lax.psum(block, axis)


def layer_norm(tokens_in):
    centred = tokens_in - jnp.mean(tokens_in, axis=-1, keepdims=True)
    spread_sq = jnp.mean(centred * centred, axis=-1, keepdims=True)
    return centred * lax.rsqrt(spread_sq + norm_eps)


def head_norm(heads_in, gain_row):
    power = jnp.mean(heads_in * heads_in, axis=-1, keepdims=True)
    return (heads_in * lax.rsqrt(power + norm_eps) * gain_row).astype(jnp.bfloat16)


def modulate_rows(hidden, modulate):
    normed = layer_norm(hidden.astype(jnp.float32))
    return (normed * (1.0 + modulate[1]) + modulate[0]).astype(jnp.bfloat16)


def pick_start(patch_slot, order, offsets, window):
    chosen = jnp.sum(jnp.where(jnp.arange(window) == patch_slot, order[:window], 0))
    picked = jnp.sum(jnp.where(jnp.arange(offsets.shape[0]) == chosen, offsets, 0))
    return picked


def attend(projected, gain_pair, cache_keys, cache_values, row_start):
    row_count = projected.shape[0]
    heads_here = projected.shape[1] // (3 * HD)
    parts_all = projected.reshape(row_count, 3, heads_here, HD)
    queries = head_norm(parts_all[:, 0], gain_pair[0])
    fresh_keys = head_norm(parts_all[:, 1], gain_pair[1])
    fresh_values = parts_all[:, 2].astype(jnp.bfloat16)
    length = cache_keys.shape[0]
    stale_keys = cache_keys.reshape(length, heads_here, HD)
    stale_values = cache_values.reshape(length, heads_here, HD)
    root_size = math.sqrt(HD)
    old_scores = (
        jnp.einsum("qhd,khd->hqk", queries, stale_keys, preferred_element_type=jnp.float32)
        / root_size
    )
    positions = lax.broadcasted_iota(jnp.int32, (1, 1, length), 2)
    replaced = (positions >= row_start) & (positions < row_start + row_count)
    old_scores = jnp.where(replaced, -jnp.inf, old_scores)
    new_scores = (
        jnp.einsum("qhd,khd->hqk", queries, fresh_keys, preferred_element_type=jnp.float32)
        / root_size
    )
    top_score = jnp.maximum(
        jnp.max(old_scores, axis=-1, keepdims=True), jnp.max(new_scores, axis=-1, keepdims=True)
    )
    old_weights = jnp.exp(old_scores - top_score)
    new_weights = jnp.exp(new_scores - top_score)
    totals = jnp.sum(old_weights, axis=-1) + jnp.sum(new_weights, axis=-1)
    mixed_sum = jnp.einsum(
        "hqk,khd->qhd",
        old_weights.astype(jnp.bfloat16),
        stale_values,
        preferred_element_type=jnp.float32,
    )
    mixed_sum = mixed_sum + jnp.einsum(
        "hqk,khd->qhd",
        new_weights.astype(jnp.bfloat16),
        fresh_values,
        preferred_element_type=jnp.float32,
    )
    attended = (mixed_sum / jnp.transpose(totals)[:, :, None]).astype(jnp.bfloat16)
    return attended.reshape(row_count, heads_here * HD)


def shards(patch_tokens, modulation, w_qkv, qk_gain, w_out, kv_cache, order, offsets):
    segment_index = lax.axis_index("pipe")
    segment_count = lax.axis_size("pipe")
    window = patch_tokens.shape[0]
    local_rows = patch_tokens.shape[1]
    model_width = patch_tokens.shape[2]
    modulate = modulation[0, 0]
    weight_in = w_qkv[0].reshape(model_width, -1)
    gain_pair = qk_gain[0]
    weight_out = w_out[0]
    cache_keys = kv_cache[0, 0, 0]
    cache_values = kv_cache[0, 0, 1]
    tick_count = window + segment_count - 1

    def project_rows(row_piece):
        return jnp.dot(row_piece, weight_in, preferred_element_type=jnp.float32)

    def finish(projected, hidden_shard, patch_slot):
        row_start = pick_start(patch_slot, order, offsets, window)
        attended = attend(projected, gain_pair, cache_keys, cache_values, row_start)
        head_total = lax.psum_scatter(
            jnp.dot(attended, weight_out, preferred_element_type=jnp.float32).astype(jnp.bfloat16),
            "sp",
            scatter_dimension=0,
            tiled=True,
        ).astype(jnp.float32)
        return (hidden_shard.astype(jnp.float32) + modulate[2] * head_total).astype(jnp.bfloat16)

    def slot_of(tick_step):
        patch_item = tick_step - segment_index
        is_valid = (patch_item >= 0) & (patch_item < window)
        return (jnp.clip(patch_item, 0, window - 1), is_valid)

    empty_store = jnp.zeros(patch_tokens.shape, jnp.bfloat16)

    def shard_tick(tick_step, carried):
        incoming, stored = carried
        patch_slot, is_valid = slot_of(tick_step)
        first_patch = lax.dynamic_index_in_dim(patch_tokens, patch_slot, 0, keepdims=False)
        hidden = jnp.where(segment_index == 0, first_patch, incoming)
        projected = project_rows(
            lax.all_gather(modulate_rows(hidden, modulate), "sp", axis=0, tiled=True)
        )
        new_shard = finish(projected, hidden, patch_slot)
        updated = lax.dynamic_update_index_in_dim(stored, new_shard, patch_slot, 0)
        stored = jnp.where(is_valid, updated, stored)
        incoming = from_behind(new_shard, "pipe", 1)
        return (incoming, stored)

    start_rows = jnp.zeros((local_rows, model_width), jnp.bfloat16)
    last_rows, stored = lax.fori_loop(0, tick_count, shard_tick, (start_rows, empty_store))
    branch_index = lax.axis_index("cfg")
    half_window = window // lax.axis_size("cfg")
    own_block = lax.dynamic_slice_in_dim(stored, branch_index * half_window, half_window, 0)
    sent_block = lax.dynamic_slice_in_dim(stored, (1 - branch_index) * half_window, half_window, 0)
    partner = from_partner(sent_block, "cfg", 0)
    on_cond = branch_index == 0
    cond_rows = jnp.where(on_cond, own_block, partner).astype(jnp.float32)
    uncond = jnp.where(on_cond, partner, own_block).astype(jnp.float32)
    guided_full = (uncond + guide_scale * (cond_rows - uncond)).astype(jnp.bfloat16)
    block_width = model_width // segment_count
    whole_guided = spread(guided_full, "pipe", segment_count - 1)
    guided = lax.dynamic_slice_in_dim(whole_guided, segment_index * block_width, block_width, 2)
    return (stored[None, None], guided)


def solution(mesh):
    return jax.shard_map(
        shards,
        mesh=mesh,
        in_specs=(
            P(None, "sp", None),
            P("pipe", "cfg", None, None),
            P("pipe", None, None, "sp"),
            P("pipe", None, None),
            P("pipe", "sp", None),
            P("pipe", "cfg", None, None, "sp"),
            P(),
            P(),
        ),
        out_specs=(P("pipe", "cfg", None, "sp", None), P("cfg", "sp", "pipe")),
        check_vma=False,
    )
```

profile of v0, /device:TPU:2, one launch (start us, length us, event | category | flops | bytes accessed | tf_op | source)
XLA Modules:
  0.0 1448.0 jit_solution(8262481205884530222)
XLA Ops:
  22.0 1337.2 %while.16 = (s32[]{:T(128)}, bf16[8,3072]{1,0:T(8,128)(2,1)S(1)}, bf16[4,8,3072]{2,1,0:T(8,128)(2,1)}, pred[]{:T(512)}, s32[]{:T(128)}, /*index=5*/bf16[4,8,3072...) while((s32[]{:T(128)}, bf16[8,3072]{1,0:T(8,128)(2,1)S(1)}, ...), condition=%wide.region_12.13_spmd, body=%wide.region_0.12_spmd.sunk | while | flops 956501184 | bytes 43381164 | solution.py:148
  24.3 23.4 %all_gather.9 = bf16[128,3072]{1,0:T(8,128)(2,1)S(1)} all-gather(bf16[8,3072]{1,0:T(8,128)(2,1)S(1)} %fusion.109), channel_id=1, replica_groups=mesh['pipe'=8,'sp'=16,'cfg'=2] {'sp'}, dimensions={0}, use_global_device_ids=true | all-gather | bytes 835584 | tf_op jit(solution)/shard_map/while/body/eval_jaxpr/all_gather | solution.py:139
  57.3 4.9 convolution_convert_fusion.2
  62.3 74.9 %reduce-scatter.2.cloned.1.call-done = bf16[8,3072]{1,0:T(8,128)(2,1)} async-done(((bf16[128,3072]{1,0:T(8,128)(2,1)}), bf16[8,3072]{1,0:T(8,128)(2,1)}) %reduce-scatter.2.cloned.1.call-update) | async-done | bytes 49168 | tf_op jit(solution)/shard_map/while/body/eval_jaxpr/reduce_scatter | solution.py:118
  146.0 21.9 %all_gather.9 = bf16[128,3072]{1,0:T(8,128)(2,1)S(1)} all-gather(bf16[8,3072]{1,0:T(8,128)(2,1)S(1)} %fusion.109), channel_id=1, replica_groups=mesh['pipe'=8,'sp'=16,'cfg'=2] {'sp'}, dimensions={0}, use_global_device_ids=true | all-gather | bytes 835584 | tf_op jit(solution)/shard_map/while/body/eval_jaxpr/all_gather | solution.py:139
  177.6 4.9 convolution_convert_fusion.2
  182.6 76.1 %reduce-scatter.2.cloned.1.call-done = bf16[8,3072]{1,0:T(8,128)(2,1)} async-done(((bf16[128,3072]{1,0:T(8,128)(2,1)}), bf16[8,3072]{1,0:T(8,128)(2,1)}) %reduce-scatter.2.cloned.1.call-update) | async-done | bytes 49168 | tf_op jit(solution)/shard_map/while/body/eval_jaxpr/reduce_scatter | solution.py:118
  267.6 21.9 %all_gather.9 = bf16[128,3072]{1,0:T(8,128)(2,1)S(1)} all-gather(bf16[8,3072]{1,0:T(8,128)(2,1)S(1)} %fusion.109), channel_id=1, replica_groups=mesh['pipe'=8,'sp'=16,'cfg'=2] {'sp'}, dimensions={0}, use_global_device_ids=true | all-gather | bytes 835584 | tf_op jit(solution)/shard_map/while/body/eval_jaxpr/all_gather | solution.py:139
  299.2 4.9 convolution_convert_fusion.2
  304.1 76.1 %reduce-scatter.2.cloned.1.call-done = bf16[8,3072]{1,0:T(8,128)(2,1)} async-done(((bf16[128,3072]{1,0:T(8,128)(2,1)}), bf16[8,3072]{1,0:T(8,128)(2,1)}) %reduce-scatter.2.cloned.1.call-update) | async-done | bytes 49168 | tf_op jit(solution)/shard_map/while/body/eval_jaxpr/reduce_scatter | solution.py:118
  389.1 21.9 %all_gather.9 = bf16[128,3072]{1,0:T(8,128)(2,1)S(1)} all-gather(bf16[8,3072]{1,0:T(8,128)(2,1)S(1)} %fusion.109), channel_id=1, replica_groups=mesh['pipe'=8,'sp'=16,'cfg'=2] {'sp'}, dimensions={0}, use_global_device_ids=true | all-gather | bytes 835584 | tf_op jit(solution)/shard_map/while/body/eval_jaxpr/all_gather | solution.py:139
  425.7 76.1 %reduce-scatter.2.cloned.1.call-done = bf16[8,3072]{1,0:T(8,128)(2,1)} async-done(((bf16[128,3072]{1,0:T(8,128)(2,1)}), bf16[8,3072]{1,0:T(8,128)(2,1)}) %reduce-scatter.2.cloned.1.call-update) | async-done | bytes 49168 | tf_op jit(solution)/shard_map/while/body/eval_jaxpr/reduce_scatter | solution.py:118
  510.7 22.0 %all_gather.9 = bf16[128,3072]{1,0:T(8,128)(2,1)S(1)} all-gather(bf16[8,3072]{1,0:T(8,128)(2,1)S(1)} %fusion.109), channel_id=1, replica_groups=mesh['pipe'=8,'sp'=16,'cfg'=2] {'sp'}, dimensions={0}, use_global_device_ids=true | all-gather | bytes 835584 | tf_op jit(solution)/shard_map/while/body/eval_jaxpr/all_gather | solution.py:139
  542.3 4.9 convolution_convert_fusion.2
  547.3 76.1 %reduce-scatter.2.cloned.1.call-done = bf16[8,3072]{1,0:T(8,128)(2,1)} async-done(((bf16[128,3072]{1,0:T(8,128)(2,1)}), bf16[8,3072]{1,0:T(8,128)(2,1)}) %reduce-scatter.2.cloned.1.call-update) | async-done | bytes 49168 | tf_op jit(solution)/shard_map/while/body/eval_jaxpr/reduce_scatter | solution.py:118
  632.2 21.9 %all_gather.9 = bf16[128,3072]{1,0:T(8,128)(2,1)S(1)} all-gather(bf16[8,3072]{1,0:T(8,128)(2,1)S(1)} %fusion.109), channel_id=1, replica_groups=mesh['pipe'=8,'sp'=16,'cfg'=2] {'sp'}, dimensions={0}, use_global_device_ids=true | all-gather | bytes 835584 | tf_op jit(solution)/shard_map/while/body/eval_jaxpr/all_gather | solution.py:139
  663.9 4.9 convolution_convert_fusion.2
  668.8 76.1 %reduce-scatter.2.cloned.1.call-done = bf16[8,3072]{1,0:T(8,128)(2,1)} async-done(((bf16[128,3072]{1,0:T(8,128)(2,1)}), bf16[8,3072]{1,0:T(8,128)(2,1)}) %reduce-scatter.2.cloned.1.call-update) | async-done | bytes 49168 | tf_op jit(solution)/shard_map/while/body/eval_jaxpr/reduce_scatter | solution.py:118
  753.8 21.9 %all_gather.9 = bf16[128,3072]{1,0:T(8,128)(2,1)S(1)} all-gather(bf16[8,3072]{1,0:T(8,128)(2,1)S(1)} %fusion.109), channel_id=1, replica_groups=mesh['pipe'=8,'sp'=16,'cfg'=2] {'sp'}, dimensions={0}, use_global_device_ids=true | all-gather | bytes 835584 | tf_op jit(solution)/shard_map/while/body/eval_jaxpr/all_gather | solution.py:139
  785.4 4.9 convolution_convert_fusion.2
  790.3 76.1 %reduce-scatter.2.cloned.1.call-done = bf16[8,3072]{1,0:T(8,128)(2,1)} async-done(((bf16[128,3072]{1,0:T(8,128)(2,1)}), bf16[8,3072]{1,0:T(8,128)(2,1)}) %reduce-scatter.2.cloned.1.call-update) | async-done | bytes 49168 | tf_op jit(solution)/shard_map/while/body/eval_jaxpr/reduce_scatter | solution.py:118
  875.3 22.0 %all_gather.9 = bf16[128,3072]{1,0:T(8,128)(2,1)S(1)} all-gather(bf16[8,3072]{1,0:T(8,128)(2,1)S(1)} %fusion.109), channel_id=1, replica_groups=mesh['pipe'=8,'sp'=16,'cfg'=2] {'sp'}, dimensions={0}, use_global_device_ids=true | all-gather | bytes 835584 | tf_op jit(solution)/shard_map/while/body/eval_jaxpr/all_gather | solution.py:139
  911.9 76.0 %reduce-scatter.2.cloned.1.call-done = bf16[8,3072]{1,0:T(8,128)(2,1)} async-done(((bf16[128,3072]{1,0:T(8,128)(2,1)}), bf16[8,3072]{1,0:T(8,128)(2,1)}) %reduce-scatter.2.cloned.1.call-update) | async-done | bytes 49168 | tf_op jit(solution)/shard_map/while/body/eval_jaxpr/reduce_scatter | solution.py:118
  996.8 21.9 %all_gather.9 = bf16[128,3072]{1,0:T(8,128)(2,1)S(1)} all-gather(bf16[8,3072]{1,0:T(8,128)(2,1)S(1)} %fusion.109), channel_id=1, replica_groups=mesh['pipe'=8,'sp'=16,'cfg'=2] {'sp'}, dimensions={0}, use_global_device_ids=true | all-gather | bytes 835584 | tf_op jit(solution)/shard_map/while/body/eval_jaxpr/all_gather | solution.py:139
  1033.4 76.1 %reduce-scatter.2.cloned.1.call-done = bf16[8,3072]{1,0:T(8,128)(2,1)} async-done(((bf16[128,3072]{1,0:T(8,128)(2,1)}), bf16[8,3072]{1,0:T(8,128)(2,1)}) %reduce-scatter.2.cloned.1.call-update) | async-done | bytes 49168 | tf_op jit(solution)/shard_map/while/body/eval_jaxpr/reduce_scatter | solution.py:118
  1118.4 21.9 %all_gather.9 = bf16[128,3072]{1,0:T(8,128)(2,1)S(1)} all-gather(bf16[8,3072]{1,0:T(8,128)(2,1)S(1)} %fusion.109), channel_id=1, replica_groups=mesh['pipe'=8,'sp'=16,'cfg'=2] {'sp'}, dimensions={0}, use_global_device_ids=true | all-gather | bytes 835584 | tf_op jit(solution)/shard_map/while/body/eval_jaxpr/all_gather | solution.py:139
  1150.0 4.9 convolution_convert_fusion.2
  1154.9 76.0 %reduce-scatter.2.cloned.1.call-done = bf16[8,3072]{1,0:T(8,128)(2,1)} async-done(((bf16[128,3072]{1,0:T(8,128)(2,1)}), bf16[8,3072]{1,0:T(8,128)(2,1)}) %reduce-scatter.2.cloned.1.call-update) | async-done | bytes 49168 | tf_op jit(solution)/shard_map/while/body/eval_jaxpr/reduce_scatter | solution.py:118
  1239.9 21.9 %all_gather.9 = bf16[128,3072]{1,0:T(8,128)(2,1)S(1)} all-gather(bf16[8,3072]{1,0:T(8,128)(2,1)S(1)} %fusion.109), channel_id=1, replica_groups=mesh['pipe'=8,'sp'=16,'cfg'=2] {'sp'}, dimensions={0}, use_global_device_ids=true | all-gather | bytes 835584 | tf_op jit(solution)/shard_map/while/body/eval_jaxpr/all_gather | solution.py:139
  1271.5 4.9 convolution_convert_fusion.2
  1276.4 76.1 %reduce-scatter.2.cloned.1.call-done = bf16[8,3072]{1,0:T(8,128)(2,1)} async-done(((bf16[128,3072]{1,0:T(8,128)(2,1)}), bf16[8,3072]{1,0:T(8,128)(2,1)}) %reduce-scatter.2.cloned.1.call-update) | async-done | bytes 49168 | tf_op jit(solution)/shard_map/while/body/eval_jaxpr/reduce_scatter | solution.py:118
  1366.3 73.3 %all-reduce.2.cloned.1.call-done = bf16[2,8,3072]{2,1,0:T(8,128)(2,1)} async-done(((bf16[2,8,3072]{2,1,0:T(8,128)(2,1)}), bf16[2,8,3072]{2,1,0:T(8,128)(2,1)}) %all-reduce.2.cloned.1.call-update) | async-done | bytes 98320 | tf_op jit(solution)/shard_map/psum | solution.py:29
  (321 shorter events, 233.8 us)
Async XLA Ops:
  16.7 5.3 copy-start.1
  16.7 5.3 copy-start.2
  16.7 5.3 copy-start.3
  16.7 5.3 copy-start.4
  22.0 115.2 %reduce-scatter.2.cloned.1.call-start = ((), (), s32[]{:S(2)}) async-start(), calls=%async_computation.2 | async-start | bytes 835584 | tf_op jit(solution)/shard_map/while/body/eval_jaxpr/reduce_scatter | solution.py:118
  54.6 1.9 copy-start
  138.6 5.2 collective-permute-start
  143.8 114.9 %reduce-scatter.2.cloned.1.call-start = ((), (), s32[]{:S(2)}) async-start(), calls=%async_computation.2 | async-start | bytes 835584 | tf_op jit(solution)/shard_map/while/body/eval_jaxpr/reduce_scatter | solution.py:118
  260.2 5.2 collective-permute-start
  265.3 114.9 %reduce-scatter.2.cloned.1.call-start = ((), (), s32[]{:S(2)}) async-start(), calls=%async_computation.2 | async-start | bytes 835584 | tf_op jit(solution)/shard_map/while/body/eval_jaxpr/reduce_scatter | solution.py:118
  381.7 5.2 collective-permute-start
  386.9 114.9 %reduce-scatter.2.cloned.1.call-start = ((), (), s32[]{:S(2)}) async-start(), calls=%async_computation.2 | async-start | bytes 835584 | tf_op jit(solution)/shard_map/while/body/eval_jaxpr/reduce_scatter | solution.py:118
  418.1 1.9 copy-start
  503.3 5.2 collective-permute-start
  508.5 114.9 %reduce-scatter.2.cloned.1.call-start = ((), (), s32[]{:S(2)}) async-start(), calls=%async_computation.2 | async-start | bytes 835584 | tf_op jit(solution)/shard_map/while/body/eval_jaxpr/reduce_scatter | solution.py:118
  539.6 1.9 copy-start
  624.8 5.2 collective-permute-start
  630.0 114.9 %reduce-scatter.2.cloned.1.call-start = ((), (), s32[]{:S(2)}) async-start(), calls=%async_computation.2 | async-start | bytes 835584 | tf_op jit(solution)/shard_map/while/body/eval_jaxpr/reduce_scatter | solution.py:118
  746.4 5.2 collective-permute-start
  751.5 114.9 %reduce-scatter.2.cloned.1.call-start = ((), (), s32[]{:S(2)}) async-start(), calls=%async_computation.2 | async-start | bytes 835584 | tf_op jit(solution)/shard_map/while/body/eval_jaxpr/reduce_scatter | solution.py:118
  867.9 5.2 collective-permute-start
  873.1 114.9 %reduce-scatter.2.cloned.1.call-start = ((), (), s32[]{:S(2)}) async-start(), calls=%async_computation.2 | async-start | bytes 835584 | tf_op jit(solution)/shard_map/while/body/eval_jaxpr/reduce_scatter | solution.py:118
  989.4 5.2 collective-permute-start
  994.6 114.9 %reduce-scatter.2.cloned.1.call-start = ((), (), s32[]{:S(2)}) async-start(), calls=%async_computation.2 | async-start | bytes 835584 | tf_op jit(solution)/shard_map/while/body/eval_jaxpr/reduce_scatter | solution.py:118
  1025.7 1.9 copy-start
  1110.9 5.2 collective-permute-start
  1116.1 114.8 %reduce-scatter.2.cloned.1.call-start = ((), (), s32[]{:S(2)}) async-start(), calls=%async_computation.2 | async-start | bytes 835584 | tf_op jit(solution)/shard_map/while/body/eval_jaxpr/reduce_scatter | solution.py:118
  1232.4 5.2 collective-permute-start
  1237.6 114.9 %reduce-scatter.2.cloned.1.call-start = ((), (), s32[]{:S(2)}) async-start(), calls=%async_computation.2 | async-start | bytes 835584 | tf_op jit(solution)/shard_map/while/body/eval_jaxpr/reduce_scatter | solution.py:118
  1354.0 5.2 collective-permute-start
  1359.2 80.4 %all-reduce.2.cloned.1.call-start = ((), (), s32[]{:S(2)}) async-start(), calls=%async_computation.1 | async-start | bytes 196608 | tf_op jit(solution)/shard_map/psum | solution.py:29
  1360.1 4.6 collective-permute-start.1
  (7 other events, 13.5 us)
Sparse Core Ops, SparseCore 0:
  62.4 74.7 reduce-scatter.1
  182.7 75.9 reduce-scatter.1
  304.3 75.9 reduce-scatter.1
  425.8 75.9 reduce-scatter.1
  547.4 75.8 reduce-scatter.1
  668.9 75.9 reduce-scatter.1
  790.5 75.8 reduce-scatter.1
  912.0 75.8 reduce-scatter.1
  1033.5 75.8 reduce-scatter.1
  1155.1 75.8 reduce-scatter.1
  1276.6 75.8 reduce-scatter.1
Sparse Core Ops, SparseCore 1:
  1366.4 73.2 all-reduce.1
where the time goes:
time: 1450 us
  waiting for transfers between devices  932 us (64%)
  blocking collectives  243 us (17%)
  matrix products  98.7 us (7%)
  other arithmetic  78.4 us (5%)
  starting transfers between devices  38.6 us (3%)
  local copies, waits for them, and re-layouts  34.3 us (2%)
  between operations  15.2 us (1%)
    reduce_scatter x11, waiting for transfers between devices, finish(): lax.psum_scatter(jnp.dot(attended, weight_out, preferred_element_type=jnp...  836 us
    all_gather x11, blocking collectives, shard_tick(): lax.all_gather(modulate_rows(hidden, modulate), 'sp', axis=0, tiled=True)  243 us
    psum x1, waiting for transfers between devices, spread(): return lax.psum(block, axis)  73.3 us
    dot_general x11, matrix products, finish(): jnp.dot(attended, weight_out, preferred_element_type=jnp.float32)  54.2 us
    ppermute x11, starting transfers between devices, from_behind(): return lax.ppermute(block, axis, route)  37.9 us
  transfers between devices with their start and end apart: 24, of which 24 were waited for; matrix products, arithmetic and copies ran while one was open for 0% of the time, Pallas kernels for 0%

commit v1 on v0

v1 whole, which is shorter than its diff:
```python
import functools
import math

import jax
import jax.numpy as jnp
from jax import lax
from jax.experimental import pallas as pl
from jax.experimental.pallas import tpu as pltpu
from jax.sharding import PartitionSpec as P

HD = 128
norm_eps = 1e-06
guide_scale = 3.5
CHUNK = 2048
WIDE = 512
SCALE = math.log2(math.e) / math.sqrt(HD)
VMEM_BYTES = 34 * 1024 * 1024


def dot(a, b):
    return jnp.dot(a, b, preferred_element_type=jnp.float32)


def dot_t(a, b):
    return lax.dot_general(a, b, (((1,), (1,)), ((), ())), preferred_element_type=jnp.float32)


def head_norm(heads_in, gain_row):
    power = jnp.mean(heads_in * heads_in, axis=-1, keepdims=True)
    return (heads_in * lax.rsqrt(power + norm_eps) * gain_row).astype(jnp.bfloat16)


def lanes_sum(total, wide):
    for b in range(wide.shape[1] // 128):
        total = total + wide[:, b * 128 : (b + 1) * 128]
    return total


def front_half(gathered, hidden_before, gate, w_out, entering, use_entering, hidden_out):
    rows, width = hidden_out.shape
    attended = jnp.concatenate([gathered[i] for i in range(gathered.shape[0])], axis=1)
    total = jnp.zeros((rows, 128), jnp.float32)
    for n in range(width // WIDE):
        cols = slice(n * WIDE, (n + 1) * WIDE)
        head_total = dot(attended, w_out[:, cols])
        before = hidden_before[:, cols].astype(jnp.float32)
        hidden = (before + gate[0:1, cols] * head_total).astype(jnp.bfloat16)
        if entering is not None:
            hidden = jnp.where(use_entering, entering[:, cols], hidden)
        hidden_out[:, cols] = hidden
        total = lanes_sum(total, hidden.astype(jnp.float32))
    return total


def back_half(
    total, hidden, modulate, w_own, w_other, gain, kv_own, kv_other, row_start, core, out, modded, scores
):
    rows, width = hidden.shape
    length = kv_own.shape[1]
    mean = jnp.sum(total, axis=1, keepdims=True) * (1.0 / width)
    spread = jnp.zeros((rows, 128), jnp.float32)
    for n in range(width // 128):
        centred = hidden[:, n * 128 : (n + 1) * 128].astype(jnp.float32) - mean
        spread = spread + centred * centred
    inverse = lax.rsqrt(jnp.sum(spread, axis=1, keepdims=True) * (1.0 / width) + norm_eps)
    for n in range(width // WIDE):
        cols = slice(n * WIDE, (n + 1) * WIDE)
        normed = (hidden[:, cols].astype(jnp.float32) - mean) * inverse
        modded[:, cols] = (normed * (1.0 + modulate[1:2, cols]) + modulate[0:1, cols]).astype(jnp.bfloat16)
    queries, fresh_keys, fresh_values = [], [], []
    for weight in (w_own, w_other):
        projected = dot(modded[...], weight[...])
        queries.append(head_norm(projected[:, :HD], gain[0:1, :]))
        fresh_keys.append(head_norm(projected[:, HD : 2 * HD], gain[1:2, :]))
        fresh_values.append(projected[:, 2 * HD :].astype(jnp.bfloat16))
    caches = (kv_own, kv_other)
    window = pl.ds(row_start, rows)
    window_block = lax.div(row_start, 128)
    steps = length // CHUNK
    lowest = jnp.full((rows, 128), -jnp.inf, jnp.float32)

    def score(head, step, top):
        part = slice(step * CHUNK, (step + 1) * CHUNK)
        old = dot_t(queries[head], caches[head][0, part, :])
        scores[head, :, part] = old
        for b in range(CHUNK // 128):
            replaced = step * (CHUNK // 128) + b == window_block
            top = jnp.maximum(top, jnp.where(replaced, -jnp.inf, old[:, b * 128 : (b + 1) * 128]))
        return top

    def start_weights(head, top):
        fresh = dot_t(queries[head], fresh_keys[head])
        scores[head, :, window] = lowest
        top = jnp.max(jnp.maximum(top, fresh), axis=1, keepdims=True)
        weights = jnp.exp2((fresh - top) * SCALE)
        return top, weights, dot(weights.astype(jnp.bfloat16), fresh_values[head])

    def weigh(head, step, top, totals, mixed):
        part = slice(step * CHUNK, (step + 1) * CHUNK)
        weights = jnp.exp2((scores[head, :, part] - top) * SCALE)
        totals = lanes_sum(totals, weights)
        return totals, mixed + dot(weights.astype(jnp.bfloat16), caches[head][1, part, :])

    top = lowest
    for step in range(steps):
        top = score(0, step, top)
    for head in range(2):
        top, totals, mixed = start_weights(head, top)
        next_top = lowest
        for step in range(steps):
            if head == 0:
                next_top = score(1, step, next_top)
            totals, mixed = weigh(head, step, top, totals, mixed)
        place = core if head == 0 else 1 - core
        cols = pl.ds(pl.multiple_of(place * HD, HD), HD)
        out[:, cols] = (mixed / jnp.sum(totals, axis=1, keepdims=True)).astype(jnp.bfloat16)
        top = next_top


def first_kernel(scal, x, mod, w_own, w_other, gain, kv_own, kv_other, out, modded, scores):
    total = jnp.zeros((x.shape[0], 128), jnp.float32)
    total = lanes_sum(total, x[...].astype(jnp.float32))
    back_half(
        total, x, mod, w_own, w_other, gain, kv_own, kv_other,
        pl.multiple_of(scal[0], 128), scal[1], out, modded, scores,
    )


def whole_kernel(has_x, scal, gathered, before, gate, w_out, *rest):
    x = rest[0] if has_x else None
    mod, w_own, w_other, gain, kv_own, kv_other, hidden, out, modded, scores = rest[has_x:]
    total = front_half(gathered, before, gate, w_out, x, scal[2] == 1, hidden)
    back_half(
        total, hidden, mod, w_own, w_other, gain, kv_own, kv_other,
        pl.multiple_of(scal[0], 128), scal[1], out, modded, scores,
    )


def last_kernel(gathered, before, gate, w_out, hidden):
    front_half(gathered, before, gate, w_out, None, None, hidden)


def call(kernel, operands, outs, scratch, scalars):
    vmem = pl.BlockSpec(memory_space=pltpu.VMEM)
    specs = [vmem] * len(operands)
    if scalars:
        specs[0] = pl.BlockSpec(memory_space=pltpu.SMEM)
    return pl.pallas_call(
        kernel,
        out_shape=outs,
        in_specs=specs,
        out_specs=tuple(vmem for _ in outs),
        scratch_shapes=scratch,
        compiler_params=pltpu.CompilerParams(vmem_limit_bytes=VMEM_BYTES),
    )(*operands)


def keep(array):
    return pltpu.with_memory_space_constraint(array, pltpu.VMEM)


def shards(patch_tokens, modulation, w_qkv, qk_gain, w_out, kv_cache, order, offsets):
    sections = lax.axis_size("pipe")
    members = lax.axis_size("sp")
    chips = members // 2
    section = lax.axis_index("pipe")
    place = lax.axis_index("sp")
    core = place % 2
    chip = place // 2
    window, own_rows, width = patch_tokens.shape
    slots = window // 2
    rows = own_rows * members
    bf16 = jnp.bfloat16

    same_core = [[2 * i + c for i in range(chips)] for c in range(2)]

    def other_core(value):
        return lax.ppermute(value, "sp", [(i, i ^ 1) for i in range(members)])

    def onward(value):
        return lax.ppermute(value, "pipe", [(i, (i + 1) % sections) for i in range(sections)])

    def back(value):
        return lax.ppermute(value, "pipe", [(i, (i - 1) % sections) for i in range(sections)])

    w_before = onward(w_out[0])
    gate_before = onward(modulation[0, 0, 2:3])
    kv_own = kv_cache[0, 0]
    kv_other = other_core(kv_own)
    w_own = w_qkv[0].reshape(width, 3 * HD)
    w_other = other_core(w_own)
    mod = modulation[0, 0, 0:2]
    gain = qk_gain[0]

    to_cores = jnp.swapaxes(patch_tokens.reshape(slots, 2, own_rows, width), 0, 1)
    to_all = jnp.broadcast_to(to_cores[None], (chips, 2, slots, own_rows, width))
    entered = lax.all_to_all(
        to_all.reshape(members, slots, own_rows, width), "sp", 0, 0, tiled=True
    )
    entering = [entered[:, k].reshape(rows, width) for k in range(slots)]

    w_all = lax.all_gather(w_before, "sp", axis=0, tiled=True)

    def start_of(patch):
        chosen = jnp.sum(jnp.where(jnp.arange(order.shape[0]) == patch, order, 0))
        return jnp.sum(jnp.where(jnp.arange(offsets.shape[0]) == chosen, offsets, 0))

    starts = [start_of(2 * k + core).astype(jnp.int32) for k in range(slots)]

    def scalars(tick):
        start = starts[0]
        for k in range(1, slots):
            start = jnp.where(tick - section >= k, starts[k], start)
        enters = (section == 0) & (tick < slots)
        return jnp.stack([start, core.astype(jnp.int32), enters.astype(jnp.int32)])

    statics = [mod, keep(w_own), keep(w_other), gain, keep(kv_own), keep(kv_other)]
    w_all = keep(w_all)
    hidden_shape = jax.ShapeDtypeStruct((rows, width), bf16)
    attended_shape = jax.ShapeDtypeStruct((rows, 2 * HD), bf16)
    scratch = [
        pltpu.VMEM((rows, width), bf16),
        pltpu.VMEM((2, rows, kv_own.shape[1]), jnp.float32),
    ]

    stored = [jnp.zeros((2 * own_rows, width), bf16) for _ in range(slots)]
    hidden = entering[0]
    (attended,) = call(
        first_kernel, [scalars(0), hidden, *statics], (attended_shape,), scratch, True
    )
    ticks = sections + slots
    for tick in range(1, ticks):
        arrived = onward(attended)
        before = onward(hidden)
        gathered = lax.all_to_all(
            jnp.broadcast_to(arrived[None], (chips, rows, 2 * HD)),
            "sp", 0, 0, axis_index_groups=same_core, tiled=True,
        )
        if tick == ticks - 1:
            (hidden,) = call(
                last_kernel, [gathered, before, gate_before, w_all], (hidden_shape,), [], False
            )
        else:
            has_x = tick < slots
            extra = [entering[tick]] if has_x else []
            hidden, attended = call(
                functools.partial(whole_kernel, has_x),
                [scalars(tick), gathered, before, gate_before, w_all, *extra, *statics],
                (hidden_shape, attended_shape), scratch, True,
            )
        chip_rows = lax.dynamic_slice_in_dim(hidden, chip * 2 * own_rows, 2 * own_rows, 0)
        ends = jnp.where(section == 0, sections, section)
        for k in range(slots):
            stored[k] = jnp.where(tick == ends + k, chip_rows, stored[k])

    both = jnp.stack(stored).reshape(slots, 2, own_rows, width)
    mine = jnp.where(core == 0, both[:, 0], both[:, 1])
    theirs = other_core(jnp.where(core == 0, both[:, 1], both[:, 0]))
    pair = jnp.where(core == 0, jnp.stack([mine, theirs], 1), jnp.stack([theirs, mine], 1))
    finished = pair.reshape(window, own_rows, width)
    section_out = back(finished)

    branches = lax.axis_size("cfg")
    part = width // sections
    pieces = finished.reshape(branches, window // branches, own_rows, sections, part)
    pieces = jnp.transpose(pieces, (3, 0, 1, 2, 4))
    pieces = pieces.reshape(sections * branches, window // branches, own_rows, part)
    landed = lax.all_to_all(pieces, ("pipe", "cfg"), 0, 0, tiled=True)
    cond = landed[0].astype(jnp.float32)
    uncond = landed[1].astype(jnp.float32)
    guided = (uncond + guide_scale * (cond - uncond)).astype(bf16)
    return (section_out[None, None], guided)


def solution(mesh):
    return jax.shard_map(
        shards,
        mesh=mesh,
        in_specs=(
            P(None, "sp", None),
            P("pipe", "cfg", None, None),
            P("pipe", None, None, "sp"),
            P("pipe", None, None),
            P("pipe", "sp", None),
            P("pipe", "cfg", None, None, "sp"),
            P(),
            P(),
        ),
        out_specs=(P("pipe", "cfg", None, "sp", None), P("cfg", "sp", "pipe")),
        check_vma=False,
    )
```

time: 1450 us -> 626 us (0.43)
  waiting for transfers between devices: 932 us -> 322 us
  blocking collectives: 243 us -> 0 us
  matrix products: 98.7 us -> 0 us
  Pallas kernels: 0 us -> 93 us
  other arithmetic: 78.4 us -> 11.8 us
  local copies, waits for them, and re-layouts: 34.3 us -> 86.8 us
  starting transfers between devices: 38.6 us -> 76.1 us
    reduce_scatter x11 -> x0, waiting for transfers between devices: 836 us -> none  [finish(): lax.psum_scatter(jnp.dot(attended, weight_out, preferred_element_type=jnp...]
    all_gather x11 -> x0, blocking collectives: 243 us -> none  [shard_tick(): lax.all_gather(modulate_rows(hidden, modulate), 'sp', axis=0, tiled=True)]
    ppermute x12 -> x24, waiting for transfers between devices: 23 us -> 198 us  [the longest x20 189 us: onward(): lax.ppermute(value, 'pipe', [(i, (i + 1) % sections) for i in range(secti...]
    dot_general x55 -> x0, matrix products: 98.7 us -> none  [the longest x11 54.2 us: finish(): jnp.dot(attended, weight_out, preferred_element_type=jnp.float32)]
    pallas_call x0 -> x10, Pallas kernels: none -> 93 us  [call(): pl.pallas_call(kernel, out_shape=outs, in_specs=specs, out_specs=tuple((v...]
    all_to_all x0 -> x11, waiting for transfers between devices: none -> 86.7 us  [the longest x9 65.2 us: shards(): lax.all_to_all(jnp.broadcast_to(arrived[None], (chips, rows, 2 * HD)), 's...]
    psum x1 -> x0, waiting for transfers between devices: 73.3 us -> none  [spread(): return lax.psum(block, axis)]
    unnamed x10 -> x71, local copies, waits for them, and re-layouts: 5.7 us -> 72.4 us
  transfers between devices with their start and end apart: 24 -> 36, of which waited for: 24 -> 25; matrix products, arithmetic and copies ran while one was open for 0% -> 4% of each run, Pallas kernels for 0% -> 1%
where the time goes in v1:
time: 626 us; the launch traced here: 616 us
  waiting for transfers between devices  322 us (51%)
  Pallas kernels  93 us (15%)
  local copies, waits for them, and re-layouts  86.8 us (14%)
  starting transfers between devices  76.1 us (12%)
  between operations  26.2 us (4%)
  other arithmetic  11.8 us (2%)
    ppermute x20, waiting for transfers between devices, onward(): lax.ppermute(value, 'pipe', [(i, (i + 1) % sections) for i in range(secti...  189 us
    pallas_call x10, Pallas kernels, call(): pl.pallas_call(kernel, out_shape=outs, in_specs=specs, out_specs=tuple((v...  93 us
    unnamed x71, local copies, waits for them, and re-layouts  72.4 us
    all_to_all x9, waiting for transfers between devices, shards(): lax.all_to_all(jnp.broadcast_to(arrived[None], (chips, rows, 2 * HD)), 's...  65.2 us
    all_to_all x9, starting transfers between devices, shards(): lax.all_to_all(jnp.broadcast_to(arrived[None], (chips, rows, 2 * HD)), 's...  52.5 us
    all_gather x1, waiting for transfers between devices, shards(): w_all = lax.all_gather(w_before, 'sp', axis=0, tiled=True)  36.9 us
    all_to_all x1, waiting for transfers between devices, shards(): lax.all_to_all(to_all.reshape(members, slots, own_rows, width), 'sp', 0,...  21 us
  transfers between devices with their start and end apart: 36, of which 25 were waited for; matrix products, arithmetic and copies ran while one was open for 4% of the time, Pallas kernels for 1%

profile of v1, /device:TPU:2, one launch (start us, length us, event | category | flops | bytes accessed | tf_op | source)
XLA Modules:
  0.0 616.0 jit_solution(17662700230535417718)
XLA Ops:
  9.2 21.7 %collective-permute-done.5 = bf16[128,3072]{1,0:T(8,128)(2,1)S(1)} collective-permute-done((bf16[128,3072]{1,0:T(8,128)(2,1)}, bf16[128,3072]{1,0:T(8,128)(2,1)S(1)}, u32[]{:S(2)}, u32[]{:S(2)}) %collective-permute-start.5) | collective-permute-done | bytes 786464 | tf_op jit(solution)/shard_map/ppermute | solution.py:181
  41.2 7.5 %all-to-all-start = ((bf16[16,2,8,3072]{3,2,1,0:T(8,128)(2,1)}), bf16[16,2,8,3072]{3,2,1,0:T(8,128)(2,1)}, u32[]{:S(2)}, u32[]{:S(2)}) async-start(bf16[16,2,8,3072]{3,2,1,0:T(8,128)(2,1)} %bitcast.91), calls=%async_computation | async-start | bytes 3145728 | tf_op jit(solution)/shard_map/all_to_all | solution.py:197
  52.8 21.0 %all-to-all-done = bf16[16,2,8,3072]{3,2,1,0:T(8,128)(2,1)} async-done(((bf16[16,2,8,3072]{3,2,1,0:T(8,128)(2,1)}), bf16[16,2,8,3072]{3,2,1,0:T(8,128)(2,1)}, u32[]{:S(2)}, u32[]{:S(2)}) %all-to-all-start) | async-done | bytes 1572896 | tf_op jit(solution)/shard_map/all_to_all | solution.py:197
  78.4 7.4 %shard_map.95 = bf16[128,256]{1,0:T(8,128)(2,1)S(1)} custom-call(s32[3]{0:T(128)S(1)} %add_add_fusion.1.scal, bf16[128,3072]{1,0:T(8,128)(2,1)S(1)} %get-tuple-element.39.x, f32[2,3072]{1,0:T(2,128)S(1)} %bitcast.72, bf16[3072,384]{1,0:T(8,128)(2,1)S(1)} %copy.46.w_own.rest_2_.rest_1_, bf16[3072,384]{1,0:T(8,128)(2,1)} %collective-permute-done.w_other.rest_3_.rest_2_, ...), custom_call_target="tpu_custom_call" | custom-call | tf_op jit(solution)/shard_map/pallas_call | solution.py:148
  93.0 7.3 %all-to-all-start.1 = ((bf16[8,128,256]{2,1,0:T(8,128)(2,1)}), bf16[8,128,256]{2,1,0:T(8,128)(2,1)}, u32[]{:S(2)}, u32[]{:S(2)}) async-start(bf16[8,128,256]{2,1,0:T(8,128)(2,1)} %broadcast_in_dim.31), calls=%async_computation.1 | async-start | bytes 1048576 | tf_op jit(solution)/shard_map/all_to_all | solution.py:235
  112.3 36.9 %all-gather.2.cloned.1.call-done.w_out = bf16[2048,3072]{1,0:T(8,128)(2,1)} async-done(((bf16[128,3072]{1,0:T(8,128)(2,1)}), bf16[2048,3072]{1,0:T(8,128)(2,1)}) %all-gather.2.cloned.1.call-update) | async-done | bytes 12582928 | tf_op jit(solution)/shard_map/all_gather | solution.py:202
  156.0 10.7 %shard_map.96 = (bf16[128,3072]{1,0:T(8,128)(2,1)}, bf16[128,256]{1,0:T(8,128)(2,1)}) custom-call(s32[3]{0:T(128)} %add_add_fusion.scal, bf16[8,128,256]{2,1,0:T(8,128)(2,1)} %all-to-all-done.1.gathered, bf16[128,3072]{1,0:T(8,128)(2,1)} %collective-permute-done.3.before, f32[1,3072]{1,0:T(1,128)} %copy-done.19, bf16[2048,3072]{1,0:T(8,128)(2,1)S(1)} %copy-done, ...), custom_call_target="tpu_custom_call" | custom-call | tf_op jit(solution)/shard_map/pallas_call | solution.py:148
  169.7 19.8 %collective-permute-done.6 = bf16[128,256]{1,0:T(8,128)(2,1)S(1)} collective-permute-done((bf16[128,256]{1,0:T(8,128)(2,1)}, bf16[128,256]{1,0:T(8,128)(2,1)S(1)}, u32[]{:S(2)}, u32[]{:S(2)}) %collective-permute-start.6) | collective-permute-done | bytes 65568 | tf_op jit(solution)/shard_map/ppermute | solution.py:181
  197.8 8.7 %all-to-all-done.2.gathered = bf16[8,128,256]{2,1,0:T(8,128)(2,1)S(1)} async-done(((bf16[8,128,256]{2,1,0:T(8,128)(2,1)}), bf16[8,128,256]{2,1,0:T(8,128)(2,1)S(1)}, u32[]{:S(2)}, u32[]{:S(2)}) %all-to-all-start.2) | async-done | bytes 524320 | tf_op jit(solution)/shard_map/all_to_all | solution.py:235
  214.1 10.4 %shard_map.97 = (bf16[128,3072]{1,0:T(8,128)(2,1)}, bf16[128,256]{1,0:T(8,128)(2,1)}) custom-call(s32[3]{0:T(128)} %pad_add_fusion.scal, bf16[8,128,256]{2,1,0:T(8,128)(2,1)} %copy-done.23, bf16[128,3072]{1,0:T(8,128)(2,1)} %collective-permute-done.7.before, f32[1,3072]{1,0:T(1,128)} %copy-done.19, bf16[2048,3072]{1,0:T(8,128)(2,1)S(1)} %copy-done.1, ...), custom_call_target="tpu_custom_call" | custom-call | tf_op jit(solution)/shard_map/pallas_call | solution.py:148
  225.7 19.6 %collective-permute-done.8 = bf16[128,256]{1,0:T(8,128)(2,1)S(1)} collective-permute-done((bf16[128,256]{1,0:T(8,128)(2,1)}, bf16[128,256]{1,0:T(8,128)(2,1)S(1)}, u32[]{:S(2)}, u32[]{:S(2)}) %collective-permute-start.8) | collective-permute-done | bytes 65568 | tf_op jit(solution)/shard_map/ppermute | solution.py:181
  254.3 7.9 %all-to-all-done.3.gathered = bf16[8,128,256]{2,1,0:T(8,128)(2,1)S(1)} async-done(((bf16[8,128,256]{2,1,0:T(8,128)(2,1)}), bf16[8,128,256]{2,1,0:T(8,128)(2,1)S(1)}, u32[]{:S(2)}, u32[]{:S(2)}) %all-to-all-start.3) | async-done | bytes 524320 | tf_op jit(solution)/shard_map/all_to_all | solution.py:235
  269.8 10.4 %shard_map.98 = (bf16[128,3072]{1,0:T(8,128)(2,1)}, bf16[128,256]{1,0:T(8,128)(2,1)}) custom-call(s32[3]{0:T(128)} %pad_add_fusion.1.scal, bf16[8,128,256]{2,1,0:T(8,128)(2,1)} %copy-done.24, bf16[128,3072]{1,0:T(8,128)(2,1)} %collective-permute-done.9.before, f32[1,3072]{1,0:T(1,128)} %copy-done.19, bf16[2048,3072]{1,0:T(8,128)(2,1)S(1)} %copy-done.2, ...), custom_call_target="tpu_custom_call" | custom-call | tf_op jit(solution)/shard_map/pallas_call | solution.py:148
  280.2 20.3 %collective-permute-done.10 = bf16[128,256]{1,0:T(8,128)(2,1)S(1)} collective-permute-done((bf16[128,256]{1,0:T(8,128)(2,1)}, bf16[128,256]{1,0:T(8,128)(2,1)S(1)}, u32[]{:S(2)}, u32[]{:S(2)}) %collective-permute-start.10) | collective-permute-done | bytes 65568 | tf_op jit(solution)/shard_map/ppermute | solution.py:181
  309.2 7.2 %all-to-all-done.4.gathered = bf16[8,128,256]{2,1,0:T(8,128)(2,1)S(1)} async-done(((bf16[8,128,256]{2,1,0:T(8,128)(2,1)}), bf16[8,128,256]{2,1,0:T(8,128)(2,1)S(1)}, u32[]{:S(2)}, u32[]{:S(2)}) %all-to-all-start.4) | async-done | bytes 524320 | tf_op jit(solution)/shard_map/all_to_all | solution.py:235
  324.0 10.4 %shard_map.99 = (bf16[128,3072]{1,0:T(8,128)(2,1)}, bf16[128,256]{1,0:T(8,128)(2,1)}) custom-call(s32[3]{0:T(128)} %pad_add_fusion.2.scal, bf16[8,128,256]{2,1,0:T(8,128)(2,1)} %copy-done.25, bf16[128,3072]{1,0:T(8,128)(2,1)} %collective-permute-done.11.before, f32[1,3072]{1,0:T(1,128)} %copy-done.19, bf16[2048,3072]{1,0:T(8,128)(2,1)S(1)} %copy-done.3, ...), custom_call_target="tpu_custom_call" | custom-call | tf_op jit(solution)/shard_map/pallas_call | solution.py:148
  334.4 19.5 %collective-permute-done.12 = bf16[128,256]{1,0:T(8,128)(2,1)S(1)} collective-permute-done((bf16[128,256]{1,0:T(8,128)(2,1)}, bf16[128,256]{1,0:T(8,128)(2,1)S(1)}, u32[]{:S(2)}, u32[]{:S(2)}) %collective-permute-start.12) | collective-permute-done | bytes 65568 | tf_op jit(solution)/shard_map/ppermute | solution.py:181
  361.9 7.1 %all-to-all-done.5.gathered = bf16[8,128,256]{2,1,0:T(8,128)(2,1)S(1)} async-done(((bf16[8,128,256]{2,1,0:T(8,128)(2,1)}), bf16[8,128,256]{2,1,0:T(8,128)(2,1)S(1)}, u32[]{:S(2)}, u32[]{:S(2)}) %all-to-all-start.5) | async-done | bytes 524320 | tf_op jit(solution)/shard_map/all_to_all | solution.py:235
  376.6 10.4 %shard_map.100 = (bf16[128,3072]{1,0:T(8,128)(2,1)}, bf16[128,256]{1,0:T(8,128)(2,1)}) custom-call(s32[3]{0:T(128)} %pad_add_fusion.3.scal, bf16[8,128,256]{2,1,0:T(8,128)(2,1)} %copy-done.26, bf16[128,3072]{1,0:T(8,128)(2,1)} %collective-permute-done.13.before, f32[1,3072]{1,0:T(1,128)} %copy-done.19, bf16[2048,3072]{1,0:T(8,128)(2,1)S(1)} %copy-done.4, ...), custom_call_target="tpu_custom_call" | custom-call | tf_op jit(solution)/shard_map/pallas_call | solution.py:148
  387.2 20.6 %collective-permute-done.14 = bf16[128,256]{1,0:T(8,128)(2,1)S(1)} collective-permute-done((bf16[128,256]{1,0:T(8,128)(2,1)}, bf16[128,256]{1,0:T(8,128)(2,1)S(1)}, u32[]{:S(2)}, u32[]{:S(2)}) %collective-permute-start.14) | collective-permute-done | bytes 65568 | tf_op jit(solution)/shard_map/ppermute | solution.py:181
  416.4 7.5 %all-to-all-done.6.gathered = bf16[8,128,256]{2,1,0:T(8,128)(2,1)S(1)} async-done(((bf16[8,128,256]{2,1,0:T(8,128)(2,1)}), bf16[8,128,256]{2,1,0:T(8,128)(2,1)S(1)}, u32[]{:S(2)}, u32[]{:S(2)}) %all-to-all-start.6) | async-done | bytes 524320 | tf_op jit(solution)/shard_map/all_to_all | solution.py:235
  431.5 10.4 %shard_map.101 = (bf16[128,3072]{1,0:T(8,128)(2,1)}, bf16[128,256]{1,0:T(8,128)(2,1)}) custom-call(s32[3]{0:T(128)} %pad_add_fusion.4.scal, bf16[8,128,256]{2,1,0:T(8,128)(2,1)} %copy-done.27, bf16[128,3072]{1,0:T(8,128)(2,1)} %collective-permute-done.15.before, f32[1,3072]{1,0:T(1,128)} %copy-done.19, bf16[2048,3072]{1,0:T(8,128)(2,1)S(1)} %copy-done.5, ...), custom_call_target="tpu_custom_call" | custom-call | tf_op jit(solution)/shard_map/pallas_call | solution.py:148
  441.9 19.8 %collective-permute-done.16 = bf16[128,256]{1,0:T(8,128)(2,1)S(1)} collective-permute-done((bf16[128,256]{1,0:T(8,128)(2,1)}, bf16[128,256]{1,0:T(8,128)(2,1)S(1)}, u32[]{:S(2)}, u32[]{:S(2)}) %collective-permute-start.16) | collective-permute-done | bytes 65568 | tf_op jit(solution)/shard_map/ppermute | solution.py:181
  462.6 6.5 %all-to-all-start.7 = ((bf16[8,128,256]{2,1,0:T(8,128)(2,1)}), bf16[8,128,256]{2,1,0:T(8,128)(2,1)S(1)}, u32[]{:S(2)}, u32[]{:S(2)}) async-start(bf16[8,128,256]{2,1,0:T(8,128)(2,1)} %broadcast_in_dim.37), calls=%async_computation.7 | async-start | bytes 1048576 | tf_op jit(solution)/shard_map/all_to_all | solution.py:235
  471.0 7.2 %all-to-all-done.7.gathered = bf16[8,128,256]{2,1,0:T(8,128)(2,1)S(1)} async-done(((bf16[8,128,256]{2,1,0:T(8,128)(2,1)}), bf16[8,128,256]{2,1,0:T(8,128)(2,1)S(1)}, u32[]{:S(2)}, u32[]{:S(2)}) %all-to-all-start.7) | async-done | bytes 524320 | tf_op jit(solution)/shard_map/all_to_all | solution.py:235
  485.8 10.4 %shard_map.102 = (bf16[128,3072]{1,0:T(8,128)(2,1)}, bf16[128,256]{1,0:T(8,128)(2,1)}) custom-call(s32[3]{0:T(128)} %pad_add_fusion.5.scal, bf16[8,128,256]{2,1,0:T(8,128)(2,1)} %copy-done.28, bf16[128,3072]{1,0:T(8,128)(2,1)} %collective-permute-done.17.before, f32[1,3072]{1,0:T(1,128)} %copy-done.19, bf16[2048,3072]{1,0:T(8,128)(2,1)S(1)} %copy-done.6, ...), custom_call_target="tpu_custom_call" | custom-call | tf_op jit(solution)/shard_map/pallas_call | solution.py:148
  496.2 19.5 %collective-permute-done.18 = bf16[128,256]{1,0:T(8,128)(2,1)S(1)} collective-permute-done((bf16[128,256]{1,0:T(8,128)(2,1)}, bf16[128,256]{1,0:T(8,128)(2,1)S(1)}, u32[]{:S(2)}, u32[]{:S(2)}) %collective-permute-start.18) | collective-permute-done | bytes 65568 | tf_op jit(solution)/shard_map/ppermute | solution.py:181
  523.6 7.1 %all-to-all-done.8.gathered = bf16[8,128,256]{2,1,0:T(8,128)(2,1)S(1)} async-done(((bf16[8,128,256]{2,1,0:T(8,128)(2,1)}), bf16[8,128,256]{2,1,0:T(8,128)(2,1)S(1)}, u32[]{:S(2)}, u32[]{:S(2)}) %all-to-all-start.8) | async-done | bytes 524320 | tf_op jit(solution)/shard_map/all_to_all | solution.py:235
  538.3 10.4 %shard_map.103 = (bf16[128,3072]{1,0:T(8,128)(2,1)}, bf16[128,256]{1,0:T(8,128)(2,1)}) custom-call(s32[3]{0:T(128)} %pad_add_fusion.6.scal, bf16[8,128,256]{2,1,0:T(8,128)(2,1)} %copy-done.22, bf16[128,3072]{1,0:T(8,128)(2,1)} %collective-permute-done.19.before, f32[1,3072]{1,0:T(1,128)} %copy-done.19, bf16[2048,3072]{1,0:T(8,128)(2,1)S(1)} %copy-done.7, ...), custom_call_target="tpu_custom_call" | custom-call | tf_op jit(solution)/shard_map/pallas_call | solution.py:148
  548.7 17.8 %collective-permute-done.20 = bf16[128,256]{1,0:T(8,128)(2,1)S(1)} collective-permute-done((bf16[128,256]{1,0:T(8,128)(2,1)}, bf16[128,256]{1,0:T(8,128)(2,1)S(1)}, u32[]{:S(2)}, u32[]{:S(2)}) %collective-permute-start.20) | collective-permute-done | bytes 65568 | tf_op jit(solution)/shard_map/ppermute | solution.py:181
  572.1 9.1 %all-to-all-done.9.gathered = bf16[8,128,256]{2,1,0:T(8,128)(2,1)S(1)} async-done(((bf16[8,128,256]{2,1,0:T(8,128)(2,1)}), bf16[8,128,256]{2,1,0:T(8,128)(2,1)S(1)}, u32[]{:S(2)}, u32[]{:S(2)}) %all-to-all-start.9) | async-done | bytes 524320 | tf_op jit(solution)/shard_map/all_to_all | solution.py:235
  599.2 7.9 %collective-permute-done.23 = bf16[4,8,3072]{2,1,0:T(8,128)(2,1)S(1)} collective-permute-done((bf16[4,8,3072]{2,1,0:T(8,128)(2,1)S(1)}, bf16[4,8,3072]{2,1,0:T(8,128)(2,1)S(1)}, u32[]{:S(2)}, u32[]{:S(2)}) %collective-permute-start.23) | collective-permute-done | bytes 196640 | tf_op jit(solution)/shard_map/ppermute | solution.py:184
  (158 shorter events, 171.1 us)
Async XLA Ops:
  7.2 142.0 %all-gather.2.cloned.1.call-start = ((), (), s32[]{:S(2)}) async-start(), calls=%async_computation.11 | async-start | bytes 13369344 | tf_op jit(solution)/shard_map/all_gather | solution.py:202
  7.2 23.7 %collective-permute-start.5 = (bf16[128,3072]{1,0:T(8,128)(2,1)}, bf16[128,3072]{1,0:T(8,128)(2,1)S(1)}, u32[]{:S(2)}, u32[]{:S(2)}) collective-permute-start(bf16[128,3072]{1,0:T(8,128)(2,1)} %bitcast.98), channel_id=1, source_target_pairs={{0,32},{32,64},{64,96},{96,128},{128,160},{160,192},{192,224},{224... | collective-permute-start | bytes 2359304 | tf_op jit(solution)/shard_map/ppermute | solution.py:181
  31.8 44.4 %collective-permute-start.1 = (bf16[2,8192,128]{2,1,0:T(8,128)(2,1)}, bf16[2,8192,128]{2,1,0:T(8,128)(2,1)}, u32[]{:S(2)}, u32[]{:S(2)}) collective-permute-start(bf16[2,8192,128]{2,1,0:T(8,128)(2,1)} %bitcast.62), channel_id=1, source_target_pairs={{0,2},{2,0},{4,6},{6,4},{8,10},{10,8},{12,14},{14,12},{16,18},{18,... | collective-permute-start | bytes 12582920 | tf_op jit(solution)/shard_map/ppermute | solution.py:178
  39.2 37.0 %collective-permute-start = (bf16[3072,384]{1,0:T(8,128)(2,1)S(1)}, bf16[3072,384]{1,0:T(8,128)(2,1)}, u32[]{:S(2)}, u32[]{:S(2)}) collective-permute-start(bf16[3072,384]{1,0:T(8,128)(2,1)S(1)} %copy.46.w_own.rest_2_.rest_1_), channel_id=1, source_target_pairs={{0,2},{2,0},{4,6},{6,4},{8,10},{10,8},{12,14},{14,12},{16,18},{18,... | collective-permute-start | bytes 7077896 | tf_op jit(solution)/shard_map/ppermute | solution.py:178
  41.2 32.6 %all-to-all-start = ((bf16[16,2,8,3072]{3,2,1,0:T(8,128)(2,1)}), bf16[16,2,8,3072]{3,2,1,0:T(8,128)(2,1)}, u32[]{:S(2)}, u32[]{:S(2)}) async-start(bf16[16,2,8,3072]{3,2,1,0:T(8,128)(2,1)} %bitcast.91), calls=%async_computation | async-start | bytes 3145728 | tf_op jit(solution)/shard_map/all_to_all | solution.py:197
  86.7 22.3 %collective-permute-start.3 = (bf16[128,3072]{1,0:T(8,128)(2,1)S(1)}, bf16[128,3072]{1,0:T(8,128)(2,1)}, u32[]{:S(2)}, u32[]{:S(2)}) collective-permute-start(bf16[128,3072]{1,0:T(8,128)(2,1)S(1)} %get-tuple-element.39.x), channel_id=1, source_target_pairs={{0,32},{32,64},{64,96},{96,128},{128,160},{160,192},{192,224},{224... | collective-permute-start | bytes 2359304 | tf_op jit(solution)/shard_map/ppermute | solution.py:181
  93.0 19.4 %all-to-all-start.1 = ((bf16[8,128,256]{2,1,0:T(8,128)(2,1)}), bf16[8,128,256]{2,1,0:T(8,128)(2,1)}, u32[]{:S(2)}, u32[]{:S(2)}) async-start(bf16[8,128,256]{2,1,0:T(8,128)(2,1)} %broadcast_in_dim.31), calls=%async_computation.1 | async-start | bytes 1048576 | tf_op jit(solution)/shard_map/all_to_all | solution.py:235
  166.6 39.9 %collective-permute-start.7 = (bf16[128,3072]{1,0:T(8,128)(2,1)}, bf16[128,3072]{1,0:T(8,128)(2,1)}, u32[]{:S(2)}, u32[]{:S(2)}) collective-permute-start(bf16[128,3072]{1,0:T(8,128)(2,1)} %get-tuple-element.19), channel_id=1, source_target_pairs={{0,32},{32,64},{64,96},{96,128},{128,160},{160,192},{192,224},{224... | collective-permute-start | bytes 2359304 | tf_op jit(solution)/shard_map/ppermute | solution.py:181
  168.2 21.3 %collective-permute-start.6 = (bf16[128,256]{1,0:T(8,128)(2,1)}, bf16[128,256]{1,0:T(8,128)(2,1)S(1)}, u32[]{:S(2)}, u32[]{:S(2)}) collective-permute-start(bf16[128,256]{1,0:T(8,128)(2,1)} %get-tuple-element.18), channel_id=1, source_target_pairs={{0,32},{32,64},{64,96},{96,128},{128,160},{160,192},{192,224},{224... | collective-permute-start | bytes 196616 | tf_op jit(solution)/shard_map/ppermute | solution.py:181
  190.3 16.2 %all-to-all-start.2 = ((bf16[8,128,256]{2,1,0:T(8,128)(2,1)}), bf16[8,128,256]{2,1,0:T(8,128)(2,1)S(1)}, u32[]{:S(2)}, u32[]{:S(2)}) async-start(bf16[8,128,256]{2,1,0:T(8,128)(2,1)} %broadcast_in_dim.32), calls=%async_computation.2 | async-start | bytes 1048576 | tf_op jit(solution)/shard_map/all_to_all | solution.py:235
  224.5 37.7 %collective-permute-start.9 = (bf16[128,3072]{1,0:T(8,128)(2,1)}, bf16[128,3072]{1,0:T(8,128)(2,1)}, u32[]{:S(2)}, u32[]{:S(2)}) collective-permute-start(bf16[128,3072]{1,0:T(8,128)(2,1)} %get-tuple-element.21), channel_id=1, source_target_pairs={{0,32},{32,64},{64,96},{96,128},{128,160},{160,192},{192,224},{224... | collective-permute-start | bytes 2359304 | tf_op jit(solution)/shard_map/ppermute | solution.py:181
  224.5 20.9 %collective-permute-start.8 = (bf16[128,256]{1,0:T(8,128)(2,1)}, bf16[128,256]{1,0:T(8,128)(2,1)S(1)}, u32[]{:S(2)}, u32[]{:S(2)}) collective-permute-start(bf16[128,256]{1,0:T(8,128)(2,1)} %get-tuple-element.20), channel_id=1, source_target_pairs={{0,32},{32,64},{64,96},{96,128},{128,160},{160,192},{192,224},{224... | collective-permute-start | bytes 196616 | tf_op jit(solution)/shard_map/ppermute | solution.py:181
  246.2 16.0 %all-to-all-start.3 = ((bf16[8,128,256]{2,1,0:T(8,128)(2,1)}), bf16[8,128,256]{2,1,0:T(8,128)(2,1)S(1)}, u32[]{:S(2)}, u32[]{:S(2)}) async-start(bf16[8,128,256]{2,1,0:T(8,128)(2,1)} %broadcast_in_dim.33), calls=%async_computation.3 | async-start | bytes 1048576 | tf_op jit(solution)/shard_map/all_to_all | solution.py:235
  280.2 36.2 %collective-permute-start.11 = (bf16[128,3072]{1,0:T(8,128)(2,1)}, bf16[128,3072]{1,0:T(8,128)(2,1)}, u32[]{:S(2)}, u32[]{:S(2)}) collective-permute-start(bf16[128,3072]{1,0:T(8,128)(2,1)} %get-tuple-element.23), channel_id=1, source_target_pairs={{0,32},{32,64},{64,96},{96,128},{128,160},{160,192},{192,224},{224... | collective-permute-start | bytes 2359304 | tf_op jit(solution)/shard_map/ppermute | solution.py:181
  280.2 20.3 %collective-permute-start.10 = (bf16[128,256]{1,0:T(8,128)(2,1)}, bf16[128,256]{1,0:T(8,128)(2,1)S(1)}, u32[]{:S(2)}, u32[]{:S(2)}) collective-permute-start(bf16[128,256]{1,0:T(8,128)(2,1)} %get-tuple-element.22), channel_id=1, source_target_pairs={{0,32},{32,64},{64,96},{96,128},{128,160},{160,192},{192,224},{224... | collective-permute-start | bytes 196616 | tf_op jit(solution)/shard_map/ppermute | solution.py:181
  301.4 15.0 %all-to-all-start.4 = ((bf16[8,128,256]{2,1,0:T(8,128)(2,1)}), bf16[8,128,256]{2,1,0:T(8,128)(2,1)S(1)}, u32[]{:S(2)}, u32[]{:S(2)}) async-start(bf16[8,128,256]{2,1,0:T(8,128)(2,1)} %broadcast_in_dim.34), calls=%async_computation.4 | async-start | bytes 1048576 | tf_op jit(solution)/shard_map/all_to_all | solution.py:235
  334.4 34.6 %collective-permute-start.13 = (bf16[128,3072]{1,0:T(8,128)(2,1)}, bf16[128,3072]{1,0:T(8,128)(2,1)}, u32[]{:S(2)}, u32[]{:S(2)}) collective-permute-start(bf16[128,3072]{1,0:T(8,128)(2,1)} %get-tuple-element.25), channel_id=1, source_target_pairs={{0,32},{32,64},{64,96},{96,128},{128,160},{160,192},{192,224},{224... | collective-permute-start | bytes 2359304 | tf_op jit(solution)/shard_map/ppermute | solution.py:181
  334.4 19.5 %collective-permute-start.12 = (bf16[128,256]{1,0:T(8,128)(2,1)}, bf16[128,256]{1,0:T(8,128)(2,1)S(1)}, u32[]{:S(2)}, u32[]{:S(2)}) collective-permute-start(bf16[128,256]{1,0:T(8,128)(2,1)} %get-tuple-element.24), channel_id=1, source_target_pairs={{0,32},{32,64},{64,96},{96,128},{128,160},{160,192},{192,224},{224... | collective-permute-start | bytes 196616 | tf_op jit(solution)/shard_map/ppermute | solution.py:181
  354.7 14.3 %all-to-all-start.5 = ((bf16[8,128,256]{2,1,0:T(8,128)(2,1)}), bf16[8,128,256]{2,1,0:T(8,128)(2,1)S(1)}, u32[]{:S(2)}, u32[]{:S(2)}) async-start(bf16[8,128,256]{2,1,0:T(8,128)(2,1)} %broadcast_in_dim.35), calls=%async_computation.5 | async-start | bytes 1048576 | tf_op jit(solution)/shard_map/all_to_all | solution.py:235
  387.1 36.8 %collective-permute-start.15 = (bf16[128,3072]{1,0:T(8,128)(2,1)}, bf16[128,3072]{1,0:T(8,128)(2,1)}, u32[]{:S(2)}, u32[]{:S(2)}) collective-permute-start(bf16[128,3072]{1,0:T(8,128)(2,1)} %get-tuple-element.27), channel_id=1, source_target_pairs={{0,32},{32,64},{64,96},{96,128},{128,160},{160,192},{192,224},{224... | collective-permute-start | bytes 2359304 | tf_op jit(solution)/shard_map/ppermute | solution.py:181
  387.1 20.7 %collective-permute-start.14 = (bf16[128,256]{1,0:T(8,128)(2,1)}, bf16[128,256]{1,0:T(8,128)(2,1)S(1)}, u32[]{:S(2)}, u32[]{:S(2)}) collective-permute-start(bf16[128,256]{1,0:T(8,128)(2,1)} %get-tuple-element.26), channel_id=1, source_target_pairs={{0,32},{32,64},{64,96},{96,128},{128,160},{160,192},{192,224},{224... | collective-permute-start | bytes 196616 | tf_op jit(solution)/shard_map/ppermute | solution.py:181
  408.6 15.3 %all-to-all-start.6 = ((bf16[8,128,256]{2,1,0:T(8,128)(2,1)}), bf16[8,128,256]{2,1,0:T(8,128)(2,1)S(1)}, u32[]{:S(2)}, u32[]{:S(2)}) async-start(bf16[8,128,256]{2,1,0:T(8,128)(2,1)} %broadcast_in_dim.36), calls=%async_computation.6 | async-start | bytes 1048576 | tf_op jit(solution)/shard_map/all_to_all | solution.py:235
  441.9 36.3 %collective-permute-start.17 = (bf16[128,3072]{1,0:T(8,128)(2,1)}, bf16[128,3072]{1,0:T(8,128)(2,1)}, u32[]{:S(2)}, u32[]{:S(2)}) collective-permute-start(bf16[128,3072]{1,0:T(8,128)(2,1)} %get-tuple-element.29), channel_id=1, source_target_pairs={{0,32},{32,64},{64,96},{96,128},{128,160},{160,192},{192,224},{224... | collective-permute-start | bytes 2359304 | tf_op jit(solution)/shard_map/ppermute | solution.py:181
  441.9 19.8 %collective-permute-start.16 = (bf16[128,256]{1,0:T(8,128)(2,1)}, bf16[128,256]{1,0:T(8,128)(2,1)S(1)}, u32[]{:S(2)}, u32[]{:S(2)}) collective-permute-start(bf16[128,256]{1,0:T(8,128)(2,1)} %get-tuple-element.28), channel_id=1, source_target_pairs={{0,32},{32,64},{64,96},{96,128},{128,160},{160,192},{192,224},{224... | collective-permute-start | bytes 196616 | tf_op jit(solution)/shard_map/ppermute | solution.py:181
  462.6 15.6 %all-to-all-start.7 = ((bf16[8,128,256]{2,1,0:T(8,128)(2,1)}), bf16[8,128,256]{2,1,0:T(8,128)(2,1)S(1)}, u32[]{:S(2)}, u32[]{:S(2)}) async-start(bf16[8,128,256]{2,1,0:T(8,128)(2,1)} %broadcast_in_dim.37), calls=%async_computation.7 | async-start | bytes 1048576 | tf_op jit(solution)/shard_map/all_to_all | solution.py:235
  496.2 34.5 %collective-permute-start.19 = (bf16[128,3072]{1,0:T(8,128)(2,1)}, bf16[128,3072]{1,0:T(8,128)(2,1)}, u32[]{:S(2)}, u32[]{:S(2)}) collective-permute-start(bf16[128,3072]{1,0:T(8,128)(2,1)} %get-tuple-element.31), channel_id=1, source_target_pairs={{0,32},{32,64},{64,96},{96,128},{128,160},{160,192},{192,224},{224... | collective-permute-start | bytes 2359304 | tf_op jit(solution)/shard_map/ppermute | solution.py:181
  496.2 19.5 %collective-permute-start.18 = (bf16[128,256]{1,0:T(8,128)(2,1)}, bf16[128,256]{1,0:T(8,128)(2,1)S(1)}, u32[]{:S(2)}, u32[]{:S(2)}) collective-permute-start(bf16[128,256]{1,0:T(8,128)(2,1)} %get-tuple-element.30), channel_id=1, source_target_pairs={{0,32},{32,64},{64,96},{96,128},{128,160},{160,192},{192,224},{224... | collective-permute-start | bytes 196616 | tf_op jit(solution)/shard_map/ppermute | solution.py:181
  516.5 14.2 %all-to-all-start.8 = ((bf16[8,128,256]{2,1,0:T(8,128)(2,1)}), bf16[8,128,256]{2,1,0:T(8,128)(2,1)S(1)}, u32[]{:S(2)}, u32[]{:S(2)}) async-start(bf16[8,128,256]{2,1,0:T(8,128)(2,1)} %broadcast_in_dim.38), calls=%async_computation.8 | async-start | bytes 1048576 | tf_op jit(solution)/shard_map/all_to_all | solution.py:235
  548.7 32.4 %collective-permute-start.21 = (bf16[128,3072]{1,0:T(8,128)(2,1)}, bf16[128,3072]{1,0:T(8,128)(2,1)S(1)}, u32[]{:S(2)}, u32[]{:S(2)}) collective-permute-start(bf16[128,3072]{1,0:T(8,128)(2,1)} %get-tuple-element.33), channel_id=1, source_target_pairs={{0,32},{32,64},{64,96},{96,128},{128,160},{160,192},{192,224},{224... | collective-permute-start | bytes 2359304 | tf_op jit(solution)/shard_map/ppermute | solution.py:181
  548.7 17.9 %collective-permute-start.20 = (bf16[128,256]{1,0:T(8,128)(2,1)}, bf16[128,256]{1,0:T(8,128)(2,1)S(1)}, u32[]{:S(2)}, u32[]{:S(2)}) collective-permute-start(bf16[128,256]{1,0:T(8,128)(2,1)} %get-tuple-element.32), channel_id=1, source_target_pairs={{0,32},{32,64},{64,96},{96,128},{128,160},{160,192},{192,224},{224... | collective-permute-start | bytes 196616 | tf_op jit(solution)/shard_map/ppermute | solution.py:181
  567.4 13.7 %all-to-all-start.9 = ((bf16[8,128,256]{2,1,0:T(8,128)(2,1)}), bf16[8,128,256]{2,1,0:T(8,128)(2,1)S(1)}, u32[]{:S(2)}, u32[]{:S(2)}) async-start(bf16[8,128,256]{2,1,0:T(8,128)(2,1)} %broadcast_in_dim.39), calls=%async_computation.9 | async-start | bytes 1048576 | tf_op jit(solution)/shard_map/all_to_all | solution.py:235
  592.4 15.2 %all-to-all-start.10 = ((bf16[16,2,8,384]{3,2,1,0:T(8,128)(2,1)}), bf16[16,2,8,384]{3,2,1,0:T(8,128)(2,1)S(1)}, u32[]{:S(2)}, u32[]{:S(2)}) async-start(bf16[16,2,8,384]{3,2,1,0:T(8,128)(2,1)} %bitcast.34), calls=%async_computation.10 | async-start | bytes 393216 | tf_op jit(solution)/shard_map/all_to_all | solution.py:268
  (39 other events, 295.5 us)
Sparse Core Ops, SparseCore 0:
  31.9 117.2 all-gather.1

commit v2 on v1

--- a/solution.py
+++ b/solution.py
@@ -14,7 +14,7 @@
 CHUNK = 2048
 WIDE = 512
 SCALE = math.log2(math.e) / math.sqrt(HD)
-VMEM_BYTES = 34 * 1024 * 1024
+VMEM_BYTES = 20 * 1024 * 1024
 
 
 def dot(a, b):
@@ -117,22 +117,22 @@
         top = next_top
 
 
-def first_kernel(scal, x, mod, w_own, w_other, gain, kv_own, kv_other, out, modded, scores):
+def first_kernel(tick, scal, x, mod, w_own, w_other, gain, kv_own, kv_other, out, modded, scores):
     total = jnp.zeros((x.shape[0], 128), jnp.float32)
     total = lanes_sum(total, x[...].astype(jnp.float32))
     back_half(
         total, x, mod, w_own, w_other, gain, kv_own, kv_other,
-        pl.multiple_of(scal[0], 128), scal[1], out, modded, scores,
-    )
-
-
-def whole_kernel(has_x, scal, gathered, before, gate, w_out, *rest):
+        pl.multiple_of(scal[2 + tick], 128), scal[0], out, modded, scores,
+    )
+
+
+def whole_kernel(tick, has_x, scal, gathered, before, gate, w_out, *rest):
     x = rest[0] if has_x else None
     mod, w_own, w_other, gain, kv_own, kv_other, hidden, out, modded, scores = rest[has_x:]
-    total = front_half(gathered, before, gate, w_out, x, scal[2] == 1, hidden)
+    total = front_half(gathered, before, gate, w_out, x, scal[1] == 0, hidden)
     back_half(
         total, hidden, mod, w_own, w_other, gain, kv_own, kv_other,
-        pl.multiple_of(scal[0], 128), scal[1], out, modded, scores,
+        pl.multiple_of(scal[2 + tick], 128), scal[0], out, modded, scores,
     )
 
 
@@ -207,12 +207,14 @@
 
     starts = [start_of(2 * k + core).astype(jnp.int32) for k in range(slots)]
 
-    def scalars(tick):
+    ticks = sections + slots
+    table = [core.astype(jnp.int32), section.astype(jnp.int32)]
+    for tick in range(ticks - 1):
         start = starts[0]
         for k in range(1, slots):
             start = jnp.where(tick - section >= k, starts[k], start)
-        enters = (section == 0) & (tick < slots)
-        return jnp.stack([start, core.astype(jnp.int32), enters.astype(jnp.int32)])
+        table.append(start)
+    scal = jnp.stack(table)
 
     statics = [mod, keep(w_own), keep(w_other), gain, keep(kv_own), keep(kv_other)]
     w_all = keep(w_all)
@@ -223,14 +225,25 @@
         pltpu.VMEM((2, rows, kv_own.shape[1]), jnp.float32),
     ]
 
-    stored = [jnp.zeros((2 * own_rows, width), bf16) for _ in range(slots)]
+    def chip_rows(hidden):
+        return lax.dynamic_slice_in_dim(hidden, chip * 2 * own_rows, 2 * own_rows, 0)
+
+    def both_patches(chip_hidden):
+        first, second = chip_hidden[:own_rows], chip_hidden[own_rows:]
+        mine = jnp.where(core == 0, first, second)
+        theirs = other_core(jnp.where(core == 0, second, first))
+        return jnp.where(core == 0, jnp.stack([mine, theirs]), jnp.stack([theirs, mine]))
+
+    ends = jnp.where(section == 0, sections, section)
+    stored = [None] * slots
+    finished = [None] * slots
     hidden = entering[0]
     (attended,) = call(
-        first_kernel, [scalars(0), hidden, *statics], (attended_shape,), scratch, True
-    )
-    ticks = sections + slots
+        functools.partial(first_kernel, 0), [scal, hidden, *statics], (attended_shape,), scratch, True
+    )
     for tick in range(1, ticks):
         arrived = onward(attended)
+        arrived, hidden = lax.optimization_barrier((arrived, hidden))
         before = onward(hidden)
         gathered = lax.all_to_all(
             jnp.broadcast_to(arrived[None], (chips, rows, 2 * HD)),
@@ -244,21 +257,21 @@
             has_x = tick < slots
             extra = [entering[tick]] if has_x else []
             hidden, attended = call(
-                functools.partial(whole_kernel, has_x),
-                [scalars(tick), gathered, before, gate_before, w_all, *extra, *statics],
+                functools.partial(whole_kernel, tick, has_x),
+                [scal, gathered, before, gate_before, w_all, *extra, *statics],
                 (hidden_shape, attended_shape), scratch, True,
             )
-        chip_rows = lax.dynamic_slice_in_dim(hidden, chip * 2 * own_rows, 2 * own_rows, 0)
-        ends = jnp.where(section == 0, sections, section)
+        held = chip_rows(hidden)
         for k in range(slots):
-            stored[k] = jnp.where(tick == ends + k, chip_rows, stored[k])
-
-    both = jnp.stack(stored).reshape(slots, 2, own_rows, width)
-    mine = jnp.where(core == 0, both[:, 0], both[:, 1])
-    theirs = other_core(jnp.where(core == 0, both[:, 1], both[:, 0]))
-    pair = jnp.where(core == 0, jnp.stack([mine, theirs], 1), jnp.stack([theirs, mine], 1))
-    finished = pair.reshape(window, own_rows, width)
-    section_out = back(finished)
+            if tick == 1 + k:
+                stored[k] = held
+            elif 1 + k < tick <= sections + k:
+                stored[k] = jnp.where(tick == ends + k, held, stored[k])
+            if tick == sections + k:
+                finished[k] = both_patches(stored[k])
+
+    section_out = jnp.concatenate([back(patches) for patches in finished])
+    finished = jnp.stack(finished)
 
     branches = lax.axis_size("cfg")
     part = width // sections

time: 626 us -> 458 us (0.73)
  waiting for transfers between devices: 322 us -> 167 us
  blocking collectives: 0 us -> 83 us
  local copies, waits for them, and re-layouts: 86.8 us -> 37 us
  starting transfers between devices: 76.1 us -> 45.4 us
  Pallas kernels: 93 us -> 84.8 us
    ppermute x20, waiting for transfers between devices: 189 us -> 93 us  [onward(): lax.ppermute(value, 'pipe', [(i, (i + 1) % sections) for i in range(secti...]
    all_to_all x0 -> x6, blocking collectives: none -> 83 us  [shards(): lax.all_to_all(jnp.broadcast_to(arrived[None], (chips, rows, 2 * HD)), 's...]
    all_to_all x9 -> x3, waiting for transfers between devices: 65.2 us -> 13.4 us  [shards(): lax.all_to_all(jnp.broadcast_to(arrived[None], (chips, rows, 2 * HD)), 's...]
    unnamed x71 -> x42, local copies, waits for them, and re-layouts: 72.4 us -> 26.7 us
    all_to_all x9 -> x3, starting transfers between devices: 52.5 us -> 16.5 us  [shards(): lax.all_to_all(jnp.broadcast_to(arrived[None], (chips, rows, 2 * HD)), 's...]
    all_to_all x1, waiting for transfers between devices: 0.51 us -> 10.2 us  [shards(): landed = lax.all_to_all(pieces, ('pipe', 'cfg'), 0, 0, tiled=True)]
    all_to_all x1, waiting for transfers between devices: 21 us -> 11.6 us  [shards(): lax.all_to_all(to_all.reshape(members, slots, own_rows, width), 'sp', 0,...]
    pallas_call x10, Pallas kernels: 93 us -> 84.8 us  [call(): pl.pallas_call(kernel, out_shape=outs, in_specs=specs, out_specs=tuple((v...]
  transfers between devices with their start and end apart: 36 -> 32, of which waited for: 25 -> 22; matrix products, arithmetic and copies ran while one was open for 4% -> 5% of each run, Pallas kernels for 1% -> 2%
where the time goes in v2:
time: 458 us; the launch traced here: 450 us
  waiting for transfers between devices  167 us (36%)
  Pallas kernels  84.8 us (19%)
  blocking collectives  83 us (18%)
  starting transfers between devices  45.4 us (10%)
  local copies, waits for them, and re-layouts  37 us (8%)
  between operations  25.4 us (6%)
  other arithmetic  6.75 us (1%)
    ppermute x20, waiting for transfers between devices, onward(): lax.ppermute(value, 'pipe', [(i, (i + 1) % sections) for i in range(secti...  93 us
    pallas_call x10, Pallas kernels, call(): pl.pallas_call(kernel, out_shape=outs, in_specs=specs, out_specs=tuple((v...  84.8 us
    all_to_all x6, blocking collectives, shards(): lax.all_to_all(jnp.broadcast_to(arrived[None], (chips, rows, 2 * HD)), 's...  83 us
    all_gather x1, waiting for transfers between devices, shards(): w_all = lax.all_gather(w_before, 'sp', axis=0, tiled=True)  36.7 us
    unnamed x42, local copies, waits for them, and re-layouts  26.7 us
    all_to_all x3, starting transfers between devices, shards(): lax.all_to_all(jnp.broadcast_to(arrived[None], (chips, rows, 2 * HD)), 's...  16.5 us
    all_to_all x3, waiting for transfers between devices, shards(): lax.all_to_all(jnp.broadcast_to(arrived[None], (chips, rows, 2 * HD)), 's...  13.4 us
    all_to_all x1, waiting for transfers between devices, shards(): lax.all_to_all(to_all.reshape(members, slots, own_rows, width), 'sp', 0,...  11.6 us
  transfers between devices with their start and end apart: 32, of which 22 were waited for; matrix products, arithmetic and copies ran while one was open for 5% of the time, Pallas kernels for 2%

profile of v2, /device:TPU:2, one launch (start us, length us, event | category | flops | bytes accessed | tf_op | source)
XLA Modules:
  0.0 449.6 jit_solution(11124660835889736827)
XLA Ops:
  9.2 21.7 %collective-permute-done.5 = bf16[128,3072]{1,0:T(8,128)(2,1)S(1)} collective-permute-done((bf16[128,3072]{1,0:T(8,128)(2,1)}, bf16[128,3072]{1,0:T(8,128)(2,1)S(1)}, u32[]{:S(2)}, u32[]{:S(2)}) %collective-permute-start.5) | collective-permute-done | bytes 786464 | tf_op jit(solution)/shard_map/ppermute | solution.py:181
  41.3 7.5 %all-to-all-start = ((bf16[16,2,8,3072]{3,2,1,0:T(8,128)(2,1)}), bf16[16,2,8,3072]{3,2,1,0:T(8,128)(2,1)}, u32[]{:S(2)}, u32[]{:S(2)}) async-start(bf16[16,2,8,3072]{3,2,1,0:T(8,128)(2,1)} %bitcast.80), calls=%async_computation | async-start | bytes 3145728 | tf_op jit(solution)/shard_map/all_to_all | solution.py:197
  62.3 11.6 %all-to-all-done = bf16[16,2,8,3072]{3,2,1,0:T(8,128)(2,1)} async-done(((bf16[16,2,8,3072]{3,2,1,0:T(8,128)(2,1)}), bf16[16,2,8,3072]{3,2,1,0:T(8,128)(2,1)}, u32[]{:S(2)}, u32[]{:S(2)}) %all-to-all-start) | async-done | bytes 1572896 | tf_op jit(solution)/shard_map/all_to_all | solution.py:197
  78.5 7.4 %shard_map.95 = bf16[128,256]{1,0:T(8,128)(2,1)S(1)} custom-call(s32[11]{0:T(128)S(1)} %stack.96.scal, bf16[128,3072]{1,0:T(8,128)(2,1)S(1)} %get-tuple-element.37.x, f32[2,3072]{1,0:T(2,128)S(1)} %bitcast.61, bf16[3072,384]{1,0:T(8,128)(2,1)S(1)} %copy.30.w_own.rest_2_.rest_1_, bf16[3072,384]{1,0:T(8,128)(2,1)} %collective-permute-done.w_other.rest_3_.rest_2_, ...), custom_call_target="tpu_custom_call" | custom-call | tf_op jit(solution)/shard_map/pallas_call | solution.py:148
  86.7 5.1 %collective-permute-done.2 = bf16[128,256]{1,0:T(8,128)(2,1)S(1)} collective-permute-done((bf16[128,256]{1,0:T(8,128)(2,1)S(1)}, bf16[128,256]{1,0:T(8,128)(2,1)S(1)}, u32[]{:S(2)}, u32[]{:S(2)}) %collective-permute-start.2) | collective-permute-done | bytes 65568 | tf_op jit(solution)/shard_map/ppermute | solution.py:181
  92.7 7.1 %all-to-all-start.1 = ((bf16[8,128,256]{2,1,0:T(8,128)(2,1)}), bf16[8,128,256]{2,1,0:T(8,128)(2,1)}, u32[]{:S(2)}, u32[]{:S(2)}) async-start(bf16[8,128,256]{2,1,0:T(8,128)(2,1)} %broadcast_in_dim.31), calls=%async_computation.1 | async-start | bytes 1048576 | tf_op jit(solution)/shard_map/all_to_all | solution.py:248
  101.6 10.9 %collective-permute-done.4.gate = f32[1,3072]{1,0:T(1,128)S(1)} collective-permute-done((f32[1,3072]{1,0:T(1,128)S(1)}, f32[1,3072]{1,0:T(1,128)S(1)}, u32[]{:S(2)}, u32[]{:S(2)}) %collective-permute-start.4) | collective-permute-done | bytes 12320 | tf_op jit(solution)/shard_map/ppermute | solution.py:181
  112.6 36.7 %all-gather.2.cloned.1.call-done.w_out = bf16[2048,3072]{1,0:T(8,128)(2,1)} async-done(((bf16[128,3072]{1,0:T(8,128)(2,1)}), bf16[2048,3072]{1,0:T(8,128)(2,1)}) %all-gather.2.cloned.1.call-update) | async-done | bytes 12582928 | tf_op jit(solution)/shard_map/all_gather | solution.py:202
  157.1 9.9 %shard_map.96 = (bf16[128,3072]{1,0:T(8,128)(2,1)S(1)}, bf16[128,256]{1,0:T(8,128)(2,1)S(1)}) custom-call(s32[11]{0:T(128)S(1)} %stack.96.scal, bf16[8,128,256]{2,1,0:T(8,128)(2,1)} %all-to-all-done.1.gathered, bf16[128,3072]{1,0:T(8,128)(2,1)} %collective-permute-done.3.before, f32[1,3072]{1,0:T(1,128)S(1)} %collective-permute-done.4.gate, ...), custom_call_target="tpu_custom_call" | custom-call | tf_op jit(solution)/shard_map/pallas_call | solution.py:148
  173.0 15.2 %all_to_all.55.gathered = bf16[8,128,256]{2,1,0:T(8,128)(2,1)S(1)} all-to-all(bf16[8,128,256]{2,1,0:T(8,128)(2,1)S(1)} %broadcast_in_dim.32), channel_id=1, replica_groups={{0,4,8,12,16,20,24,28},{2,6,10,14,18,22,26,30},{1,5,9,13,17,21,25,29},{..., dimensions={0} | all-to-all | bytes 1048576 | tf_op jit(solution)/shard_map/all_to_all | solution.py:248
  188.2 5.2 %collective-permute-done.7.before = bf16[128,3072]{1,0:T(8,128)(2,1)S(1)} collective-permute-done((bf16[128,3072]{1,0:T(8,128)(2,1)S(1)}, bf16[128,3072]{1,0:T(8,128)(2,1)S(1)}, u32[]{:S(2)}, u32[]{:S(2)}) %collective-permute-start.7) | collective-permute-done | bytes 786464 | tf_op jit(solution)/shard_map/ppermute | solution.py:181
  193.4 9.3 %shard_map.97 = (bf16[128,3072]{1,0:T(8,128)(2,1)S(1)}, bf16[128,256]{1,0:T(8,128)(2,1)S(1)}) custom-call(s32[11]{0:T(128)S(1)} %stack.96.scal, bf16[8,128,256]{2,1,0:T(8,128)(2,1)S(1)} %all_to_all.55.gathered, bf16[128,3072]{1,0:T(8,128)(2,1)S(1)} %collective-permute-done.7.before, f32[1,3072]{1,0:T(1,128)S(1)} %collective-permute-done.4.gate, ...), custom_call_target="tpu_custom_call" | custom-call | tf_op jit(solution)/shard_map/pallas_call | solution.py:148
  202.8 5.5 %collective-permute-done.8 = bf16[128,256]{1,0:T(8,128)(2,1)S(1)} collective-permute-done((bf16[128,256]{1,0:T(8,128)(2,1)S(1)}, bf16[128,256]{1,0:T(8,128)(2,1)S(1)}, u32[]{:S(2)}, u32[]{:S(2)}) %collective-permute-start.8) | collective-permute-done | bytes 65568 | tf_op jit(solution)/shard_map/ppermute | solution.py:181
  208.3 13.8 %all_to_all.56.gathered = bf16[8,128,256]{2,1,0:T(8,128)(2,1)S(1)} all-to-all(bf16[8,128,256]{2,1,0:T(8,128)(2,1)S(1)} %broadcast_in_dim.33), channel_id=1, replica_groups={{0,4,8,12,16,20,24,28},{2,6,10,14,18,22,26,30},{1,5,9,13,17,21,25,29},{..., dimensions={0} | all-to-all | bytes 1048576 | tf_op jit(solution)/shard_map/all_to_all | solution.py:248
  226.7 9.3 %shard_map.98 = (bf16[128,3072]{1,0:T(8,128)(2,1)S(1)}, bf16[128,256]{1,0:T(8,128)(2,1)S(1)}) custom-call(s32[11]{0:T(128)S(1)} %stack.96.scal, bf16[8,128,256]{2,1,0:T(8,128)(2,1)S(1)} %all_to_all.56.gathered, bf16[128,3072]{1,0:T(8,128)(2,1)S(1)} %collective-permute-done.9.before, f32[1,3072]{1,0:T(1,128)S(1)} %collective-permute-done.4.gate, ...), custom_call_target="tpu_custom_call" | custom-call | tf_op jit(solution)/shard_map/pallas_call | solution.py:148
  236.1 6.0 %collective-permute-done.10 = bf16[128,256]{1,0:T(8,128)(2,1)S(1)} collective-permute-done((bf16[128,256]{1,0:T(8,128)(2,1)S(1)}, bf16[128,256]{1,0:T(8,128)(2,1)S(1)}, u32[]{:S(2)}, u32[]{:S(2)}) %collective-permute-start.10) | collective-permute-done | bytes 65568 | tf_op jit(solution)/shard_map/ppermute | solution.py:181
  242.1 13.5 %all_to_all.57.gathered = bf16[8,128,256]{2,1,0:T(8,128)(2,1)S(1)} all-to-all(bf16[8,128,256]{2,1,0:T(8,128)(2,1)S(1)} %broadcast_in_dim.34), channel_id=1, replica_groups={{0,4,8,12,16,20,24,28},{2,6,10,14,18,22,26,30},{1,5,9,13,17,21,25,29},{..., dimensions={0} | all-to-all | bytes 1048576 | tf_op jit(solution)/shard_map/all_to_all | solution.py:248
  258.4 9.3 %shard_map.99 = (bf16[128,3072]{1,0:T(8,128)(2,1)S(1)}, bf16[128,256]{1,0:T(8,128)(2,1)S(1)}) custom-call(s32[11]{0:T(128)S(1)} %stack.96.scal, bf16[8,128,256]{2,1,0:T(8,128)(2,1)S(1)} %all_to_all.57.gathered, bf16[128,3072]{1,0:T(8,128)(2,1)S(1)} %collective-permute-done.11.before, f32[1,3072]{1,0:T(1,128)S(1)} %collective-permute-done.4.gate, ...), custom_call_target="tpu_custom_call" | custom-call | tf_op jit(solution)/shard_map/pallas_call | solution.py:148
  267.9 6.2 %collective-permute-done.12 = bf16[128,256]{1,0:T(8,128)(2,1)S(1)} collective-permute-done((bf16[128,256]{1,0:T(8,128)(2,1)S(1)}, bf16[128,256]{1,0:T(8,128)(2,1)S(1)}, u32[]{:S(2)}, u32[]{:S(2)}) %collective-permute-start.12) | collective-permute-done | bytes 65568 | tf_op jit(solution)/shard_map/ppermute | solution.py:181
  274.2 13.6 %all_to_all.58.gathered = bf16[8,128,256]{2,1,0:T(8,128)(2,1)S(1)} all-to-all(bf16[8,128,256]{2,1,0:T(8,128)(2,1)S(1)} %broadcast_in_dim.35), channel_id=1, replica_groups={{0,4,8,12,16,20,24,28},{2,6,10,14,18,22,26,30},{1,5,9,13,17,21,25,29},{..., dimensions={0} | all-to-all | bytes 1048576 | tf_op jit(solution)/shard_map/all_to_all | solution.py:248
  288.3 9.3 %shard_map.100 = (bf16[128,3072]{1,0:T(8,128)(2,1)S(1)}, bf16[128,256]{1,0:T(8,128)(2,1)S(1)}) custom-call(s32[11]{0:T(128)S(1)} %stack.96.scal, bf16[8,128,256]{2,1,0:T(8,128)(2,1)S(1)} %all_to_all.58.gathered, bf16[128,3072]{1,0:T(8,128)(2,1)S(1)} %collective-permute-done.13.before, f32[1,3072]{1,0:T(1,128)S(1)} %collective-permute-done.4.gate, ...), custom_call_target="tpu_custom_call" | custom-call | tf_op jit(solution)/shard_map/pallas_call | solution.py:148
  297.7 6.2 %collective-permute-done.14 = bf16[128,256]{1,0:T(8,128)(2,1)S(1)} collective-permute-done((bf16[128,256]{1,0:T(8,128)(2,1)S(1)}, bf16[128,256]{1,0:T(8,128)(2,1)S(1)}, u32[]{:S(2)}, u32[]{:S(2)}) %collective-permute-start.14) | collective-permute-done | bytes 65568 | tf_op jit(solution)/shard_map/ppermute | solution.py:181
  304.0 13.6 %all_to_all.59.gathered = bf16[8,128,256]{2,1,0:T(8,128)(2,1)S(1)} all-to-all(bf16[8,128,256]{2,1,0:T(8,128)(2,1)S(1)} %broadcast_in_dim.36), channel_id=1, replica_groups={{0,4,8,12,16,20,24,28},{2,6,10,14,18,22,26,30},{1,5,9,13,17,21,25,29},{..., dimensions={0} | all-to-all | bytes 1048576 | tf_op jit(solution)/shard_map/all_to_all | solution.py:248
  317.6 9.3 %shard_map.101 = (bf16[128,3072]{1,0:T(8,128)(2,1)S(1)}, bf16[128,256]{1,0:T(8,128)(2,1)S(1)}) custom-call(s32[11]{0:T(128)S(1)} %stack.96.scal, bf16[8,128,256]{2,1,0:T(8,128)(2,1)S(1)} %all_to_all.59.gathered, bf16[128,3072]{1,0:T(8,128)(2,1)S(1)} %collective-permute-done.15.before, f32[1,3072]{1,0:T(1,128)S(1)} %collective-permute-done.4.gate, ...), custom_call_target="tpu_custom_call" | custom-call | tf_op jit(solution)/shard_map/pallas_call | solution.py:148
  327.3 6.0 %collective-permute-done.16 = bf16[128,256]{1,0:T(8,128)(2,1)S(1)} collective-permute-done((bf16[128,256]{1,0:T(8,128)(2,1)S(1)}, bf16[128,256]{1,0:T(8,128)(2,1)S(1)}, u32[]{:S(2)}, u32[]{:S(2)}) %collective-permute-start.16) | collective-permute-done | bytes 65568 | tf_op jit(solution)/shard_map/ppermute | solution.py:181
  333.3 13.4 %all_to_all.60.gathered = bf16[8,128,256]{2,1,0:T(8,128)(2,1)S(1)} all-to-all(bf16[8,128,256]{2,1,0:T(8,128)(2,1)S(1)} %broadcast_in_dim.37), channel_id=1, replica_groups={{0,4,8,12,16,20,24,28},{2,6,10,14,18,22,26,30},{1,5,9,13,17,21,25,29},{..., dimensions={0} | all-to-all | bytes 1048576 | tf_op jit(solution)/shard_map/all_to_all | solution.py:248
  346.7 9.3 %shard_map.102 = (bf16[128,3072]{1,0:T(8,128)(2,1)}, bf16[128,256]{1,0:T(8,128)(2,1)S(1)}) custom-call(s32[11]{0:T(128)S(1)} %stack.96.scal, bf16[8,128,256]{2,1,0:T(8,128)(2,1)S(1)} %all_to_all.60.gathered, bf16[128,3072]{1,0:T(8,128)(2,1)S(1)} %collective-permute-done.17.before, f32[1,3072]{1,0:T(1,128)S(1)} %collective-permute-done.4.gate, ...), custom_call_target="tpu_custom_call" | custom-call | tf_op jit(solution)/shard_map/pallas_call | solution.py:148
  356.7 4.9 %collective-permute-done.18 = bf16[128,256]{1,0:T(8,128)(2,1)S(1)} collective-permute-done((bf16[128,256]{1,0:T(8,128)(2,1)S(1)}, bf16[128,256]{1,0:T(8,128)(2,1)S(1)}, u32[]{:S(2)}, u32[]{:S(2)}) %collective-permute-start.18) | collective-permute-done | bytes 65568 | tf_op jit(solution)/shard_map/ppermute | solution.py:181
  367.3 9.0 %all-to-all-done.8.gathered = bf16[8,128,256]{2,1,0:T(8,128)(2,1)S(1)} async-done(((bf16[8,128,256]{2,1,0:T(8,128)(2,1)}), bf16[8,128,256]{2,1,0:T(8,128)(2,1)S(1)}, u32[]{:S(2)}, u32[]{:S(2)}) %all-to-all-start.8) | async-done | bytes 524320 | tf_op jit(solution)/shard_map/all_to_all | solution.py:248
  383.1 9.6 %shard_map.103 = (bf16[128,3072]{1,0:T(8,128)(2,1)}, bf16[128,256]{1,0:T(8,128)(2,1)S(1)}) custom-call(s32[11]{0:T(128)S(1)} %stack.96.scal, bf16[8,128,256]{2,1,0:T(8,128)(2,1)S(1)} %all-to-all-done.8.gathered, bf16[128,3072]{1,0:T(8,128)(2,1)} %collective-permute-done.19.before, f32[1,3072]{1,0:T(1,128)S(1)} %collective-permute-done.4.gate, ...), custom_call_target="tpu_custom_call" | custom-call | tf_op jit(solution)/shard_map/pallas_call | solution.py:148
  426.0 5.1 %all-to-all-start.10 = ((bf16[16,2,8,384]{3,2,1,0:T(8,128)(2,1)}), bf16[16,2,8,384]{3,2,1,0:T(8,128)(2,1)S(1)}, u32[]{:S(2)}, u32[]{:S(2)}) async-start(bf16[16,2,8,384]{3,2,1,0:T(8,128)(2,1)} %bitcast.32), calls=%async_computation.10 | async-start | bytes 393216 | tf_op jit(solution)/shard_map/all_to_all | solution.py:281
  431.8 10.2 %all-to-all-done.10 = bf16[16,2,8,384]{3,2,1,0:T(8,128)(2,1)S(1)} async-done(((bf16[16,2,8,384]{3,2,1,0:T(8,128)(2,1)}), bf16[16,2,8,384]{3,2,1,0:T(8,128)(2,1)S(1)}, u32[]{:S(2)}, u32[]{:S(2)}) %all-to-all-start.10) | async-done | bytes 196640 | tf_op jit(solution)/shard_map/all_to_all | solution.py:281
  (122 shorter events, 93.3 us)
Async XLA Ops:
  7.2 142.1 %all-gather.2.cloned.1.call-start = ((), (), s32[]{:S(2)}) async-start(), calls=%async_computation.11 | async-start | bytes 13369344 | tf_op jit(solution)/shard_map/all_gather | solution.py:202
  7.2 23.7 %collective-permute-start.5 = (bf16[128,3072]{1,0:T(8,128)(2,1)}, bf16[128,3072]{1,0:T(8,128)(2,1)S(1)}, u32[]{:S(2)}, u32[]{:S(2)}) collective-permute-start(bf16[128,3072]{1,0:T(8,128)(2,1)} %bitcast.90), channel_id=1, source_target_pairs={{0,32},{32,64},{64,96},{96,128},{128,160},{160,192},{192,224},{224... | collective-permute-start | bytes 2359304 | tf_op jit(solution)/shard_map/ppermute | solution.py:181
  31.8 44.5 %collective-permute-start.1 = (bf16[2,8192,128]{2,1,0:T(8,128)(2,1)}, bf16[2,8192,128]{2,1,0:T(8,128)(2,1)}, u32[]{:S(2)}, u32[]{:S(2)}) collective-permute-start(bf16[2,8192,128]{2,1,0:T(8,128)(2,1)} %bitcast.51), channel_id=1, source_target_pairs={{0,2},{2,0},{4,6},{6,4},{8,10},{10,8},{12,14},{14,12},{16,18},{18,... | collective-permute-start | bytes 12582920 | tf_op jit(solution)/shard_map/ppermute | solution.py:178
  39.3 37.0 %collective-permute-start = (bf16[3072,384]{1,0:T(8,128)(2,1)S(1)}, bf16[3072,384]{1,0:T(8,128)(2,1)}, u32[]{:S(2)}, u32[]{:S(2)}) collective-permute-start(bf16[3072,384]{1,0:T(8,128)(2,1)S(1)} %copy.30.w_own.rest_2_.rest_1_), channel_id=1, source_target_pairs={{0,2},{2,0},{4,6},{6,4},{8,10},{10,8},{12,14},{14,12},{16,18},{18,... | collective-permute-start | bytes 7077896 | tf_op jit(solution)/shard_map/ppermute | solution.py:178
  41.3 32.6 %all-to-all-start = ((bf16[16,2,8,3072]{3,2,1,0:T(8,128)(2,1)}), bf16[16,2,8,3072]{3,2,1,0:T(8,128)(2,1)}, u32[]{:S(2)}, u32[]{:S(2)}) async-start(bf16[16,2,8,3072]{3,2,1,0:T(8,128)(2,1)} %bitcast.80), calls=%async_computation | async-start | bytes 3145728 | tf_op jit(solution)/shard_map/all_to_all | solution.py:197
  85.9 5.9 %collective-permute-start.2 = (bf16[128,256]{1,0:T(8,128)(2,1)S(1)}, bf16[128,256]{1,0:T(8,128)(2,1)S(1)}, u32[]{:S(2)}, u32[]{:S(2)}) collective-permute-start(bf16[128,256]{1,0:T(8,128)(2,1)S(1)} %shard_map.95), channel_id=1, source_target_pairs={{0,32},{32,64},{64,96},{96,128},{128,160},{160,192},{192,224},{224... | collective-permute-start | bytes 196616 | tf_op jit(solution)/shard_map/ppermute | solution.py:181
  91.8 20.7 %collective-permute-start.3 = (bf16[128,3072]{1,0:T(8,128)(2,1)S(1)}, bf16[128,3072]{1,0:T(8,128)(2,1)}, u32[]{:S(2)}, u32[]{:S(2)}) collective-permute-start(bf16[128,3072]{1,0:T(8,128)(2,1)S(1)} %get-tuple-element.37.x), channel_id=1, source_target_pairs={{0,32},{32,64},{64,96},{96,128},{128,160},{160,192},{192,224},{224... | collective-permute-start | bytes 2359304 | tf_op jit(solution)/shard_map/ppermute | solution.py:181
  92.7 19.9 %all-to-all-start.1 = ((bf16[8,128,256]{2,1,0:T(8,128)(2,1)}), bf16[8,128,256]{2,1,0:T(8,128)(2,1)}, u32[]{:S(2)}, u32[]{:S(2)}) async-start(bf16[8,128,256]{2,1,0:T(8,128)(2,1)} %broadcast_in_dim.31), calls=%async_computation.1 | async-start | bytes 1048576 | tf_op jit(solution)/shard_map/all_to_all | solution.py:248
  99.8 12.8 %collective-permute-start.4 = (f32[1,3072]{1,0:T(1,128)S(1)}, f32[1,3072]{1,0:T(1,128)S(1)}, u32[]{:S(2)}, u32[]{:S(2)}) collective-permute-start(f32[1,3072]{1,0:T(1,128)S(1)} %slice_bitcast_fusion.4), channel_id=1, source_target_pairs={{0,32},{32,64},{64,96},{96,128},{128,160},{160,192},{192,224},{224... | collective-permute-start | bytes 36872 | tf_op jit(solution)/shard_map/ppermute | solution.py:181
  167.1 5.9 %collective-permute-start.6 = (bf16[128,256]{1,0:T(8,128)(2,1)S(1)}, bf16[128,256]{1,0:T(8,128)(2,1)S(1)}, u32[]{:S(2)}, u32[]{:S(2)}) collective-permute-start(bf16[128,256]{1,0:T(8,128)(2,1)S(1)} %get-tuple-element.38), channel_id=1, source_target_pairs={{0,32},{32,64},{64,96},{96,128},{128,160},{160,192},{192,224},{224... | collective-permute-start | bytes 196616 | tf_op jit(solution)/shard_map/ppermute | solution.py:181
  172.9 20.4 %collective-permute-start.7 = (bf16[128,3072]{1,0:T(8,128)(2,1)S(1)}, bf16[128,3072]{1,0:T(8,128)(2,1)S(1)}, u32[]{:S(2)}, u32[]{:S(2)}) collective-permute-start(bf16[128,3072]{1,0:T(8,128)(2,1)S(1)} %get-tuple-element.41), channel_id=1, source_target_pairs={{0,32},{32,64},{64,96},{96,128},{128,160},{160,192},{192,224},{224... | collective-permute-start | bytes 2359304 | tf_op jit(solution)/shard_map/ppermute | solution.py:181
  202.7 5.6 %collective-permute-start.8 = (bf16[128,256]{1,0:T(8,128)(2,1)S(1)}, bf16[128,256]{1,0:T(8,128)(2,1)S(1)}, u32[]{:S(2)}, u32[]{:S(2)}) collective-permute-start(bf16[128,256]{1,0:T(8,128)(2,1)S(1)} %get-tuple-element.42), channel_id=1, source_target_pairs={{0,32},{32,64},{64,96},{96,128},{128,160},{160,192},{192,224},{224... | collective-permute-start | bytes 196616 | tf_op jit(solution)/shard_map/ppermute | solution.py:181
  208.3 18.4 %collective-permute-start.9 = (bf16[128,3072]{1,0:T(8,128)(2,1)S(1)}, bf16[128,3072]{1,0:T(8,128)(2,1)S(1)}, u32[]{:S(2)}, u32[]{:S(2)}) collective-permute-start(bf16[128,3072]{1,0:T(8,128)(2,1)S(1)} %get-tuple-element.45), channel_id=1, source_target_pairs={{0,32},{32,64},{64,96},{96,128},{128,160},{160,192},{192,224},{224... | collective-permute-start | bytes 2359304 | tf_op jit(solution)/shard_map/ppermute | solution.py:181
  236.0 6.1 %collective-permute-start.10 = (bf16[128,256]{1,0:T(8,128)(2,1)S(1)}, bf16[128,256]{1,0:T(8,128)(2,1)S(1)}, u32[]{:S(2)}, u32[]{:S(2)}) collective-permute-start(bf16[128,256]{1,0:T(8,128)(2,1)S(1)} %get-tuple-element.46), channel_id=1, source_target_pairs={{0,32},{32,64},{64,96},{96,128},{128,160},{160,192},{192,224},{224... | collective-permute-start | bytes 196616 | tf_op jit(solution)/shard_map/ppermute | solution.py:181
  242.1 16.3 %collective-permute-start.11 = (bf16[128,3072]{1,0:T(8,128)(2,1)S(1)}, bf16[128,3072]{1,0:T(8,128)(2,1)S(1)}, u32[]{:S(2)}, u32[]{:S(2)}) collective-permute-start(bf16[128,3072]{1,0:T(8,128)(2,1)S(1)} %get-tuple-element.49), channel_id=1, source_target_pairs={{0,32},{32,64},{64,96},{96,128},{128,160},{160,192},{192,224},{224... | collective-permute-start | bytes 2359304 | tf_op jit(solution)/shard_map/ppermute | solution.py:181
  267.8 6.3 %collective-permute-start.12 = (bf16[128,256]{1,0:T(8,128)(2,1)S(1)}, bf16[128,256]{1,0:T(8,128)(2,1)S(1)}, u32[]{:S(2)}, u32[]{:S(2)}) collective-permute-start(bf16[128,256]{1,0:T(8,128)(2,1)S(1)} %get-tuple-element.50), channel_id=1, source_target_pairs={{0,32},{32,64},{64,96},{96,128},{128,160},{160,192},{192,224},{224... | collective-permute-start | bytes 196616 | tf_op jit(solution)/shard_map/ppermute | solution.py:181
  274.1 14.2 %collective-permute-start.13 = (bf16[128,3072]{1,0:T(8,128)(2,1)S(1)}, bf16[128,3072]{1,0:T(8,128)(2,1)S(1)}, u32[]{:S(2)}, u32[]{:S(2)}) collective-permute-start(bf16[128,3072]{1,0:T(8,128)(2,1)S(1)} %get-tuple-element.53), channel_id=1, source_target_pairs={{0,32},{32,64},{64,96},{96,128},{128,160},{160,192},{192,224},{224... | collective-permute-start | bytes 2359304 | tf_op jit(solution)/shard_map/ppermute | solution.py:181
  297.6 6.3 %collective-permute-start.14 = (bf16[128,256]{1,0:T(8,128)(2,1)S(1)}, bf16[128,256]{1,0:T(8,128)(2,1)S(1)}, u32[]{:S(2)}, u32[]{:S(2)}) collective-permute-start(bf16[128,256]{1,0:T(8,128)(2,1)S(1)} %get-tuple-element.54), channel_id=1, source_target_pairs={{0,32},{32,64},{64,96},{96,128},{128,160},{160,192},{192,224},{224... | collective-permute-start | bytes 196616 | tf_op jit(solution)/shard_map/ppermute | solution.py:181
  304.0 13.6 %collective-permute-start.15 = (bf16[128,3072]{1,0:T(8,128)(2,1)S(1)}, bf16[128,3072]{1,0:T(8,128)(2,1)S(1)}, u32[]{:S(2)}, u32[]{:S(2)}) collective-permute-start(bf16[128,3072]{1,0:T(8,128)(2,1)S(1)} %get-tuple-element.57), channel_id=1, source_target_pairs={{0,32},{32,64},{64,96},{96,128},{128,160},{160,192},{192,224},{224... | collective-permute-start | bytes 2359304 | tf_op jit(solution)/shard_map/ppermute | solution.py:181
  327.0 6.3 %collective-permute-start.16 = (bf16[128,256]{1,0:T(8,128)(2,1)S(1)}, bf16[128,256]{1,0:T(8,128)(2,1)S(1)}, u32[]{:S(2)}, u32[]{:S(2)}) collective-permute-start(bf16[128,256]{1,0:T(8,128)(2,1)S(1)} %get-tuple-element.58), channel_id=1, source_target_pairs={{0,32},{32,64},{64,96},{96,128},{128,160},{160,192},{192,224},{224... | collective-permute-start | bytes 196616 | tf_op jit(solution)/shard_map/ppermute | solution.py:181
  333.3 13.4 %collective-permute-start.17 = (bf16[128,3072]{1,0:T(8,128)(2,1)S(1)}, bf16[128,3072]{1,0:T(8,128)(2,1)S(1)}, u32[]{:S(2)}, u32[]{:S(2)}) collective-permute-start(bf16[128,3072]{1,0:T(8,128)(2,1)S(1)} %get-tuple-element.61), channel_id=1, source_target_pairs={{0,32},{32,64},{64,96},{96,128},{128,160},{160,192},{192,224},{224... | collective-permute-start | bytes 2359304 | tf_op jit(solution)/shard_map/ppermute | solution.py:181
  356.1 5.6 %collective-permute-start.18 = (bf16[128,256]{1,0:T(8,128)(2,1)S(1)}, bf16[128,256]{1,0:T(8,128)(2,1)S(1)}, u32[]{:S(2)}, u32[]{:S(2)}) collective-permute-start(bf16[128,256]{1,0:T(8,128)(2,1)S(1)} %get-tuple-element.62), channel_id=1, source_target_pairs={{0,32},{32,64},{64,96},{96,128},{128,160},{160,192},{192,224},{224... | collective-permute-start | bytes 196616 | tf_op jit(solution)/shard_map/ppermute | solution.py:181
  361.6 14.7 %collective-permute-start.19 = (bf16[128,3072]{1,0:T(8,128)(2,1)}, bf16[128,3072]{1,0:T(8,128)(2,1)}, u32[]{:S(2)}, u32[]{:S(2)}) collective-permute-start(bf16[128,3072]{1,0:T(8,128)(2,1)} %get-tuple-element.65), channel_id=1, source_target_pairs={{0,32},{32,64},{64,96},{96,128},{128,160},{160,192},{192,224},{224... | collective-permute-start | bytes 2359304 | tf_op jit(solution)/shard_map/ppermute | solution.py:181
  362.5 13.8 %all-to-all-start.8 = ((bf16[8,128,256]{2,1,0:T(8,128)(2,1)}), bf16[8,128,256]{2,1,0:T(8,128)(2,1)S(1)}, u32[]{:S(2)}, u32[]{:S(2)}) async-start(bf16[8,128,256]{2,1,0:T(8,128)(2,1)} %broadcast_in_dim.38), calls=%async_computation.8 | async-start | bytes 1048576 | tf_op jit(solution)/shard_map/all_to_all | solution.py:248
  392.7 5.6 %collective-permute-start.22 = (bf16[128,256]{1,0:T(8,128)(2,1)S(1)}, bf16[128,256]{1,0:T(8,128)(2,1)S(1)}, u32[]{:S(2)}, u32[]{:S(2)}) collective-permute-start(bf16[128,256]{1,0:T(8,128)(2,1)S(1)} %get-tuple-element.67), channel_id=1, source_target_pairs={{0,32},{32,64},{64,96},{96,128},{128,160},{160,192},{192,224},{224... | collective-permute-start | bytes 196616 | tf_op jit(solution)/shard_map/ppermute | solution.py:181
  398.3 14.5 %collective-permute-start.23 = (bf16[128,3072]{1,0:T(8,128)(2,1)}, bf16[128,3072]{1,0:T(8,128)(2,1)S(1)}, u32[]{:S(2)}, u32[]{:S(2)}) collective-permute-start(bf16[128,3072]{1,0:T(8,128)(2,1)} %get-tuple-element.69), channel_id=1, source_target_pairs={{0,32},{32,64},{64,96},{96,128},{128,160},{160,192},{192,224},{224... | collective-permute-start | bytes 2359304 | tf_op jit(solution)/shard_map/ppermute | solution.py:181
  399.1 13.7 %all-to-all-start.9 = ((bf16[8,128,256]{2,1,0:T(8,128)(2,1)}), bf16[8,128,256]{2,1,0:T(8,128)(2,1)S(1)}, u32[]{:S(2)}, u32[]{:S(2)}) async-start(bf16[8,128,256]{2,1,0:T(8,128)(2,1)} %broadcast_in_dim.39), calls=%async_computation.9 | async-start | bytes 1048576 | tf_op jit(solution)/shard_map/all_to_all | solution.py:248
  403.7 1.3 collective-permute-start.20
  405.1 26.0 %collective-permute-start.21 = (bf16[2,8,3072]{2,1,0:T(8,128)(2,1)S(1)}, bf16[2,8,3072]{2,1,0:T(8,128)(2,1)S(1)}, u32[]{:S(2)}, u32[]{:S(2)}) collective-permute-start(bf16[2,8,3072]{2,1,0:T(8,128)(2,1)S(1)} %maximum_select_fusion), channel_id=1, source_target_pairs={{0,224},{32,0},{64,32},{96,64},{128,96},{160,128},{192,160},{224,1... | collective-permute-start | bytes 294920 | tf_op jit(solution)/shard_map/ppermute | solution.py:184
  420.6 1.3 collective-permute-start.24
  421.9 9.2 %collective-permute-start.25 = (bf16[2,8,3072]{2,1,0:T(8,128)(2,1)S(1)}, bf16[2,8,3072]{2,1,0:T(8,128)(2,1)S(1)}, u32[]{:S(2)}, u32[]{:S(2)}) collective-permute-start(bf16[2,8,3072]{2,1,0:T(8,128)(2,1)S(1)} %maximum_select_fusion.1), channel_id=1, source_target_pairs={{0,224},{32,0},{64,32},{96,64},{128,96},{160,128},{192,160},{224,1... | collective-permute-start | bytes 294920 | tf_op jit(solution)/shard_map/ppermute | solution.py:184
  426.0 16.1 %all-to-all-start.10 = ((bf16[16,2,8,384]{3,2,1,0:T(8,128)(2,1)}), bf16[16,2,8,384]{3,2,1,0:T(8,128)(2,1)S(1)}, u32[]{:S(2)}, u32[]{:S(2)}) async-start(bf16[16,2,8,384]{3,2,1,0:T(8,128)(2,1)} %bitcast.32), calls=%async_computation.10 | async-start | bytes 393216 | tf_op jit(solution)/shard_map/all_to_all | solution.py:281
  (21 other events, 317.4 us)
Sparse Core Ops, SparseCore 0:
  31.9 117.2 all-gather.1
